TPU v7x, 128 devices: a whole 4x4x4 slice. The times are simulated.
128 devices in a mesh: chan: 8 (over z, y_hi), win: 16 (over x, y_lo, core).
Axes of the slice: x: 4, y: 4 (y_hi: 2, y_lo: 2; y = y_hi * 2 + y_lo), z: 4, core: 2. Of those that a mesh axis runs over, the one named last changes fastest.
Arguments:
- records: bfloat16 [2048, 163840], P('chan', 'win'), may hold values from -50 to 50
- fir_taps: float32 [64], replicated, may hold values from -0.75 to 0.75
- plan: int32 [2, 8], replicated, may hold values from 0 to 7, as said below
Outputs:
- cross: float32 [64, 2, 2, 256, 2048], P('win', None, None, None, 'chan')
Inputs may be any that keep to these rules, and one draw needn't show every extreme that they name: `plan`: in each round block c is paired with block c XOR k for one nonzero key k, the same k for all blocks of the round; the rounds use different keys.
All inputs are finite; a program needn't handle non-finite values.
Results may differ from a plain program's by a relative error of at most 0.02.
Values may be sent and summed in bfloat16 or wider, within the bound.
No kernel may reach another device: no remote copies, remote signals or barrier semaphores. Data moves between devices by JAX's collectives and lax.ppermute only.
A program may use at most 128 MiB of HBM per device.

v0:
```python
import math

import jax
import jax.numpy as jnp
from jax import lax
from jax.sharding import PartitionSpec as P

WL = 256
F = 64
TAPS = 64
ROUNDS = 2


def shifted(array, axis, by):
    count = lax.axis_size(axis)
    pairs = [(i, i + by) for i in range(count) if 0 <= i + by < count]
    return lax.ppermute(array, axis, pairs)


def from_partner(block, axis, bit):
    count = lax.axis_size(axis)
    route = []
    for low in range(count):
        high = low | 1 << bit
        if high != low and high < count:
            route += [(low, high), (high, low)]
    return lax.ppermute(block, axis, route)


def fir_matrix(fir_taps):
    inputs_at = jnp.arange(WL + TAPS - 1, dtype=jnp.int32)[:, None]
    outputs_at = jnp.arange(WL, dtype=jnp.int32)[None, :]
    tap_number = outputs_at + (TAPS - 1) - inputs_at
    inside = (tap_number >= 0) & (tap_number < TAPS)
    picked = fir_taps[jnp.clip(tap_number, 0, TAPS - 1)]
    return jnp.where(inside, picked, jnp.zeros_like(picked))


def dft_table():
    sample_at = jnp.arange(WL, dtype=jnp.int32)[:, None]
    column_at = jnp.arange(2 * F, dtype=jnp.int32)[None, :]
    bin_number = column_at // 2 + 1
    phases = (sample_at * bin_number % WL).astype(jnp.float32) * (2.0 * math.pi / WL)
    return jnp.where(column_at % 2 == 0, jnp.cos(phases), -jnp.sin(phases))


def partner_layer(spectra_list):
    layers = []
    for spectra in spectra_list:
        rotated = jnp.stack([-spectra[:, 1], spectra[:, 0]], axis=1)
        layers.append(spectra)
        layers.append(rotated)
    return jnp.concatenate(layers, axis=3)


def cross_term(partner_piece, own_piece, scale):
    product = lax.dot_general(
        partner_piece,
        own_piece,
        (((1, 2), (1, 2)), ((0,), (0,))),
        preferred_element_type=jnp.float32,
    )
    return product * scale


def on_device(records, fir_taps, plan):
    channels, samples_here = records.shape
    window_count = samples_here // WL
    previous_tail = shifted(records[:, samples_here - TAPS + 1 :], "win", 1)
    samples = records.reshape(channels, window_count, WL)
    previous = jnp.concatenate(
        [previous_tail[:, None, :], samples[:, :-1, WL - TAPS + 1 :]], axis=1
    )
    combined_table = jnp.dot(fir_matrix(fir_taps), dft_table(), precision=lax.Precision.HIGHEST)
    stacked = jnp.einsum(
        "cwi,ik->kwc",
        samples.astype(jnp.float32),
        combined_table[TAPS - 1 :],
        precision=lax.Precision.HIGHEST,
    )
    stacked = stacked + jnp.einsum(
        "cwi,ik->kwc",
        previous.astype(jnp.float32),
        combined_table[: TAPS - 1],
        precision=lax.Precision.HIGHEST,
    )
    band_power = jnp.mean(stacked * stacked, axis=0, keepdims=True) + 1e-06
    whitened = (
        (stacked / jnp.sqrt(band_power)).astype(jnp.bfloat16).reshape(F, 2, window_count, channels)
    )
    device_index = lax.axis_index("chan")
    bit_count = lax.axis_size("chan").bit_length() - 1
    win_size = lax.axis_size("win")
    scale = 1.0 / math.sqrt(window_count * win_size)
    chosen = []
    images = [whitened]
    for bit_place in range(bit_count):
        images = images + [from_partner(image, "chan", bit_place) for image in images]
    for round_index in range(ROUNDS):
        offset = jnp.bitwise_xor(plan[round_index, device_index], device_index)
        picked = images[1]
        for key_value in range(2, len(images)):
            picked = jnp.where(offset == key_value, images[key_value], picked)
        chosen.append(picked)
    partner_rows = partner_layer(chosen)
    summed = lax.psum_scatter(
        cross_term(partner_rows, whitened, scale).astype(jnp.bfloat16),
        "win",
        scatter_dimension=0,
        tiled=True,
    ).astype(jnp.float32)
    return summed.reshape(summed.shape[0], ROUNDS, 2, channels, channels)


def solution(mesh):
    placed = (P("chan", "win"), P(), P())
    return jax.shard_map(
        on_device,
        mesh=mesh,
        in_specs=placed,
        out_specs=P("win", None, None, None, "chan"),
        check_vma=False,
    )
```

profile of v0, /device:TPU:1, one launch (start us, length us, event | category | flops | bytes accessed | tf_op | source)
XLA Modules:
  0.0 1222.3 jit_solution(11321515835113209890)
XLA Ops:
  6.5 7.9 copy.12
  15.2 4.6 collective-permute-start
  20.1 453.5 %gather_fusion = f32[81664]{0:T(1024)S(1)} fusion(f32[64]{0:T(128)S(1)} %copy-done, s32[81920]{0:T(1024)S(1)} %pad_clamp_fusion), kind=kCustom, calls=%fused_computation | custom fusion | bytes 979968 | tf_op jit(solution)/shard_map/gather | solution.py:35
  473.7 1.0 fusion.17
  474.7 5.2 fusion.31
  479.9 2.1 slice.37
  482.0 2.9 fusion.12
  485.5 3.0 copy.24
  488.5 2.6 collective-permute-start.1
  491.1 1.6 collective-permute-start.4
  492.7 54.8 %collective-permute-done.1 = bf16[64,2,40,256]{3,2,1,0:T(8,128)(2,1)S(1)} collective-permute-done((bf16[64,2,40,256]{3,2,1,0:T(8,128)(2,1)}, bf16[64,2,40,256]{3,2,1,0:T(8,128)(2,1)S(1)}, u32[]{:S(2)}, u32[]{:S(2)}) %collective-permute-start.1) | collective-permute-done | bytes 2621472 | tf_op jit(solution)/shard_map/ppermute | solution.py:27
  547.6 2.0 collective-permute-start.2
  549.5 3.3 collective-permute-start.7
  552.9 3.0 collective-permute-start.5
  555.8 51.2 %collective-permute-done.2 = bf16[64,2,40,256]{3,2,1,0:T(8,128)(2,1)} collective-permute-done((bf16[64,2,40,256]{3,2,1,0:T(8,128)(2,1)S(1)}, bf16[64,2,40,256]{3,2,1,0:T(8,128)(2,1)}, u32[]{:S(2)}, u32[]{:S(2)}) %collective-permute-start.2) | collective-permute-done | bytes 2621472 | tf_op jit(solution)/shard_map/ppermute | solution.py:27
  607.0 3.2 collective-permute-start.3
  612.3 54.0 %collective-permute-done.7 = bf16[64,2,40,256]{3,2,1,0:T(8,128)(2,1)} collective-permute-done((bf16[64,2,40,256]{3,2,1,0:T(8,128)(2,1)}, bf16[64,2,40,256]{3,2,1,0:T(8,128)(2,1)}, u32[]{:S(2)}, u32[]{:S(2)}) %collective-permute-start.7) | collective-permute-done | bytes 2621472 | tf_op jit(solution)/shard_map/ppermute | solution.py:27
  666.3 112.4 %collective-permute-done.5 = bf16[64,2,40,256]{3,2,1,0:T(8,128)(2,1)} collective-permute-done((bf16[64,2,40,256]{3,2,1,0:T(8,128)(2,1)}, bf16[64,2,40,256]{3,2,1,0:T(8,128)(2,1)}, u32[]{:S(2)}, u32[]{:S(2)}) %collective-permute-start.5) | collective-permute-done | bytes 2621472 | tf_op jit(solution)/shard_map/ppermute | solution.py:27
  778.6 56.2 %collective-permute-done.3 = bf16[64,2,40,256]{3,2,1,0:T(8,128)(2,1)} collective-permute-done((bf16[64,2,40,256]{3,2,1,0:T(8,128)(2,1)}, bf16[64,2,40,256]{3,2,1,0:T(8,128)(2,1)}, u32[]{:S(2)}, u32[]{:S(2)}) %collective-permute-start.3) | collective-permute-done | bytes 2621472 | tf_op jit(solution)/shard_map/ppermute | solution.py:27
  834.8 6.8 select_select_fusion.1
  841.6 2.4 slice_negate_fusion
  844.7 18.2 %fusion = bf16[64,1024,256]{2,1,0:T(8,128)(2,1)} fusion(bf16[64,2,40,256]{3,2,1,0:T(8,128)(2,1)} %bitcast.10, bf16[64,1,40,256]{3,2,1,0:T(8,128)(2,1)} %get-tuple-element.10, bf16[64,1,40,256]{3,2,1,0:T(8,128)(2,1)} %get-tuple-element.9, bf16[64,2,40,256]{3,2,1,0:T(8,128)(2,1)} %copy-done.2, bf16[64,1,40,256]{3,2,1,0:T(8,128)(2,1)} %get-tuple-element.15, ...), kind=kOutput, calls=%fused_computation.2 | convolution fusion | flops 2780823552 | bytes 46661632 | tf_op jit(solution)/shard_map/dot_general | solution.py:57
  862.9 348.5 %reduce-scatter.2.cloned.1.call-done = bf16[4,1024,256]{2,1,0:T(8,128)(2,1)} async-done(((bf16[64,1024,256]{2,1,0:T(8,128)(2,1)}), bf16[4,1024,256]{2,1,0:T(8,128)(2,1)}) %reduce-scatter.2.cloned.1.call-update) | async-done | bytes 2097168 | tf_op jit(solution)/shard_map/reduce_scatter | solution.py:106
  1211.4 4.1 convert.1
  (27 shorter events, 3.0 us)
Async XLA Ops:
  6.5 13.5 %copy-start = (f32[64]{0:T(128)S(1)}, f32[64]{0:T(128)}, u32[]{:S(2)}) copy-start(f32[64]{0:T(128)} %param.4) | copy-start | bytes 772
  6.5 1204.9 %reduce-scatter.2.cloned.1.call-start = ((), (), s32[]{:S(2)}) async-start(), calls=%async_computation.1 | async-start | bytes 35651584 | tf_op jit(solution)/shard_map/reduce_scatter | solution.py:106
  15.2 466.7 %collective-permute-start = (bf16[256,63]{0,1:T(8,128)(2,1)S(1)}, bf16[256,63]{0,1:T(8,128)(2,1)S(1)}, u32[]{:S(2)}, u32[]{:S(2)}) collective-permute-start(bf16[256,63]{0,1:T(8,128)(2,1)S(1)} %slice.36), channel_id=1, source_target_pairs={{0,1},{1,2},{2,3},{3,4},{4,5},{5,6},{6,7},{7,8},{8,9},{9,10},{10,1... | collective-permute-start | bytes 96776 | tf_op jit(solution)/shard_map/ppermute | solution.py:17
  485.5 124.7 %copy-start.4 = (s32[2,8]{1,0:T(2,128)S(1)}, s32[2,8]{1,0:T(2,128)}, u32[]{:S(2)}) copy-start(s32[2,8]{1,0:T(2,128)} %param.5) | copy-start | bytes 196
  488.5 59.1 %collective-permute-start.1 = (bf16[64,2,40,256]{3,2,1,0:T(8,128)(2,1)}, bf16[64,2,40,256]{3,2,1,0:T(8,128)(2,1)S(1)}, u32[]{:S(2)}, u32[]{:S(2)}) collective-permute-start(bf16[64,2,40,256]{3,2,1,0:T(8,128)(2,1)} %bitcast.10), channel_id=1, source_target_pairs={{0,16},{16,0},{32,48},{48,32},{64,80},{80,64},{96,112},{112,96},{1... | collective-permute-start | bytes 7864328 | tf_op jit(solution)/shard_map/ppermute | solution.py:27
  491.1 61.8 %collective-permute-start.4 = (bf16[64,2,40,256]{3,2,1,0:T(8,128)(2,1)}, bf16[64,2,40,256]{3,2,1,0:T(8,128)(2,1)}, u32[]{:S(2)}, u32[]{:S(2)}) collective-permute-start(bf16[64,2,40,256]{3,2,1,0:T(8,128)(2,1)} %bitcast.10), channel_id=1, source_target_pairs={{0,32},{32,0},{16,48},{48,16},{64,96},{96,64},{80,112},{112,80},{1... | collective-permute-start | bytes 7864328 | tf_op jit(solution)/shard_map/ppermute | solution.py:27
  547.6 231.1 %copy-start.3 = (bf16[64,2,40,256]{3,2,1,0:T(8,128)(2,1)}, bf16[64,2,40,256]{3,2,1,0:T(8,128)(2,1)S(1)}, u32[]{:S(2)}) copy-start(bf16[64,2,40,256]{3,2,1,0:T(8,128)(2,1)S(1)} %collective-permute-done.1) | copy-start | bytes 7864324
  547.6 59.5 %collective-permute-start.2 = (bf16[64,2,40,256]{3,2,1,0:T(8,128)(2,1)S(1)}, bf16[64,2,40,256]{3,2,1,0:T(8,128)(2,1)}, u32[]{:S(2)}, u32[]{:S(2)}) collective-permute-start(bf16[64,2,40,256]{3,2,1,0:T(8,128)(2,1)S(1)} %collective-permute-done.1), channel_id=1, source_target_pairs={{0,32},{32,0},{16,48},{48,16},{64,96},{96,64},{80,112},{112,80},{1... | collective-permute-start | bytes 7864328 | tf_op jit(solution)/shard_map/ppermute | solution.py:27
  549.5 116.7 %collective-permute-start.7 = (bf16[64,2,40,256]{3,2,1,0:T(8,128)(2,1)}, bf16[64,2,40,256]{3,2,1,0:T(8,128)(2,1)}, u32[]{:S(2)}, u32[]{:S(2)}) collective-permute-start(bf16[64,2,40,256]{3,2,1,0:T(8,128)(2,1)} %bitcast.10), channel_id=1, source_target_pairs={{0,64},{64,0},{16,80},{80,16},{32,96},{96,32},{48,112},{112,48},{1... | collective-permute-start | bytes 7864328 | tf_op jit(solution)/shard_map/ppermute | solution.py:27
  552.9 225.7 %collective-permute-start.6 = (bf16[64,2,40,256]{3,2,1,0:T(8,128)(2,1)S(1)}, bf16[64,2,40,256]{3,2,1,0:T(8,128)(2,1)}, u32[]{:S(2)}, u32[]{:S(2)}) collective-permute-start(bf16[64,2,40,256]{3,2,1,0:T(8,128)(2,1)S(1)} %collective-permute-done.1), channel_id=1, source_target_pairs={{0,64},{64,0},{16,80},{80,16},{32,96},{96,32},{48,112},{112,48},{1... | collective-permute-start | bytes 7864328 | tf_op jit(solution)/shard_map/ppermute | solution.py:27
  552.9 225.7 %collective-permute-start.5 = (bf16[64,2,40,256]{3,2,1,0:T(8,128)(2,1)}, bf16[64,2,40,256]{3,2,1,0:T(8,128)(2,1)}, u32[]{:S(2)}, u32[]{:S(2)}) collective-permute-start(bf16[64,2,40,256]{3,2,1,0:T(8,128)(2,1)} %collective-permute-done.4), channel_id=1, source_target_pairs={{0,64},{64,0},{16,80},{80,16},{32,96},{96,32},{48,112},{112,48},{1... | collective-permute-start | bytes 7864328 | tf_op jit(solution)/shard_map/ppermute | solution.py:27
  607.0 227.7 %collective-permute-start.3 = (bf16[64,2,40,256]{3,2,1,0:T(8,128)(2,1)}, bf16[64,2,40,256]{3,2,1,0:T(8,128)(2,1)}, u32[]{:S(2)}, u32[]{:S(2)}) collective-permute-start(bf16[64,2,40,256]{3,2,1,0:T(8,128)(2,1)} %collective-permute-done.2), channel_id=1, source_target_pairs={{0,64},{64,0},{16,80},{80,16},{32,96},{96,32},{48,112},{112,48},{1... | collective-permute-start | bytes 7864328 | tf_op jit(solution)/shard_map/ppermute | solution.py:27
  841.6 3.1 copy-start.2
  1211.4 4.1 copy-start.1
Sparse Core Ops, SparseCore 0:
  863.0 348.3 reduce-scatter.1
where the time goes:
time: 1220 us
  waiting for transfers between devices  677 us (55%)
  local copies, waits for them, and re-layouts  469 us (38%)
  matrix products  27.2 us (2%)
  starting transfers between devices  20.3 us (2%)
  between operations  15 us (1%)
  other arithmetic  14.1 us (1%)
    gather x2, local copies, waits for them, and re-layouts, fir_matrix(): picked = fir_taps[jnp.clip(tap_number, 0, TAPS - 1)]  454 us
    reduce_scatter x1, waiting for transfers between devices, on_device(): lax.psum_scatter(cross_term(partner_rows, whitened, scale).astype(jnp.bfl...  349 us
    ppermute x7, waiting for transfers between devices, from_partner(): return lax.ppermute(block, axis, route)  329 us
  transfers between devices with their start and end apart: 9, of which 6 were waited for; matrix products, arithmetic and copies ran while one was open for 38% of the time, Pallas kernels for 0%

commit v1 on v0

v1 whole, which is shorter than its diff:
```python
import functools
import math

import jax
import jax.numpy as jnp
import numpy as np
from jax import lax
from jax.experimental import pallas as pl
from jax.experimental.pallas import tpu as pltpu
from jax.sharding import Mesh
from jax.sharding import PartitionSpec as P

WL = 256
F = 64
TAPS = 64
ROUNDS = 2
STEP_WINDOWS = 8
PIECES = 3
ROWS = 80
TILE = 16
VMEM = 48 * 1024 * 1024


def dft_rows(chips, blocks):
    place = np.arange(F)
    bin_number = blocks * (place % chips) + place // chips + 1
    phase = np.arange(WL)[None, :] * bin_number[:, None] % WL * (2.0 * math.pi / WL)
    return np.concatenate([np.cos(phase), -np.sin(phase)]).astype(np.float32)


def in_pieces(table):
    pieces = []
    rest = table
    for _ in range(PIECES):
        piece = rest.astype(jnp.bfloat16)
        pieces.append(piece)
        rest = rest - piece.astype(jnp.float32)
    return jnp.concatenate(pieces, axis=0)


def table_kernel(taps_ref, dft_ref, table_ref):
    lane = lax.broadcasted_iota(jnp.int32, (1, 2 * WL), 1)
    reversed_taps = jnp.zeros((1, 2 * WL), jnp.float32)
    for tap in range(TAPS):
        reversed_taps = jnp.where(lane == TAPS - 1 - tap, taps_ref[tap], reversed_taps)
    spread = jnp.broadcast_to(reversed_taps, (WL, 2 * WL))
    toeplitz = pltpu.roll(spread, WL - TAPS + 1, 1, stride=1, stride_axis=0)
    combined = jnp.dot(
        dft_ref[...], toeplitz, precision=lax.Precision.HIGHEST, preferred_element_type=jnp.float32
    )
    count = PIECES * 2 * F
    table_ref[:count, :] = in_pieces(combined[:, WL:])
    table_ref[count:, :] = in_pieces(combined[:, :WL])


def make_table(fir_taps, dft):
    return pl.pallas_call(
        table_kernel,
        out_shape=jax.ShapeDtypeStruct((2 * PIECES * 2 * F, WL), jnp.bfloat16),
        in_specs=[pl.BlockSpec(memory_space=pltpu.SMEM), pl.BlockSpec(memory_space=pltpu.VMEM)],
        out_specs=pl.BlockSpec(memory_space=pltpu.VMEM),
        compiler_params=pltpu.CompilerParams(vmem_limit_bytes=VMEM),
        name="table",
    )(fir_taps, dft)


def add_pieces(rows):
    count = 2 * F
    total = rows[(PIECES - 1) * count : PIECES * count]
    for piece in range(PIECES - 2, -1, -1):
        total = total + rows[piece * count : (piece + 1) * count]
    return total


NT = (((1,), (1,)), ((), ()))


def spectra_kernel(tail_ref, table_ref, records_ref, out_ref, carry_ref, held_ref):
    step = pl.program_id(0)
    count = PIECES * 2 * F

    @pl.when(step == 0)
    def _():
        rows = lax.dot_general(
            table_ref[count:, WL // 2 :], tail_ref[...], NT, preferred_element_type=jnp.float32
        )
        carry_ref[...] = add_pieces(rows)

    carry = carry_ref[...]
    for inner in range(STEP_WINDOWS):
        window = step * STEP_WINDOWS + inner
        samples = records_ref[:, inner * WL : (inner + 1) * WL]
        rows = lax.dot_general(table_ref[...], samples, NT, preferred_element_type=jnp.float32)
        stacked = add_pieces(rows[:count]) + carry
        carry = add_pieces(rows[count:])
        power = jnp.sum(stacked * stacked, axis=0, keepdims=True) * (1.0 / (2 * F)) + 1e-06
        white = stacked * (1.0 / jnp.sqrt(power))
        imag_at = jnp.where(window >= 32, window + 8, window + 48)
        for half in range(2):
            lanes = pl.ds(half * 128, 128)
            part = white[:, half * 128 : (half + 1) * 128]
            held_ref[pl.ds(half * F * ROWS + window, F, stride=ROWS), :] = part[:F]
            held_ref[pl.ds(half * F * ROWS + imag_at, F, stride=ROWS), :] = part[F:]
    carry_ref[...] = carry

    @pl.when(step == pl.num_programs(0) - 1)
    def _():
        @pl.loop(0, F)
        def _(place):
            for half in range(2):
                start = pl.multiple_of(half * F * ROWS + place * ROWS, 8)
                out_ref[place, :, half * 128 : (half + 1) * 128] = held_ref[pl.ds(start, ROWS), :].astype(
                    jnp.bfloat16
                )


def spectra(tail, table, records):
    channels, samples = records.shape
    steps = samples // WL // STEP_WINDOWS
    return pl.pallas_call(
        spectra_kernel,
        grid=(steps,),
        out_shape=jax.ShapeDtypeStruct((F, ROWS, channels), jnp.bfloat16),
        in_specs=[
            pl.BlockSpec(tail.shape, lambda i: (0, 0)),
            pl.BlockSpec(table.shape, lambda i: (0, 0)),
            pl.BlockSpec((channels, STEP_WINDOWS * WL), lambda i: (0, i)),
        ],
        out_specs=pl.BlockSpec((F, ROWS, channels), lambda i: (0, 0, 0)),
        scratch_shapes=[
            pltpu.VMEM((2 * F, channels), jnp.float32),
            pltpu.VMEM((2 * F * ROWS, 128), jnp.float32),
        ],
        compiler_params=pltpu.CompilerParams(vmem_limit_bytes=VMEM),
        name="spectra",
    )(tail, table, records)


def rotated(rows):
    layers = []
    for start in range(0, rows.shape[0], ROWS):
        first, second, mixed, fourth, fifth = (
            rows[start + TILE * t : start + TILE * (t + 1)] for t in range(5)
        )
        wide = mixed.astype(jnp.float32)
        turned = jnp.concatenate([wide[8:], -wide[:8]], axis=0).astype(jnp.bfloat16)
        layers += [fourth, fifth, turned, -first, -second]
    return jnp.concatenate(layers, axis=0)


TN = (((0,), (0,)), ((), ()))


def cross_kernel(scale, plan_ref, core_ref, own_ref, own_other_ref, mate_ref, mate_other_ref, out_ref):
    del plan_ref, core_ref
    own = jnp.concatenate([own_ref[0], own_other_ref[0]], axis=0)
    mate = jnp.concatenate([mate_ref[0], mate_other_ref[0]], axis=0)
    out_ref[0, 0] = (
        lax.dot_general(mate, own, TN, preferred_element_type=jnp.float32) * scale
    ).astype(jnp.bfloat16)
    out_ref[0, 1] = (
        lax.dot_general(mate, rotated(own), TN, preferred_element_type=jnp.float32) * scale
    ).astype(jnp.bfloat16)


def cross(plan, core, here, other, scale):
    blocks, depth, channels = here.shape
    own = pl.BlockSpec((1, depth, channels), lambda c, plan_ref, core_ref: (c, 0, 0))
    mate = pl.BlockSpec((1, depth, channels), lambda c, plan_ref, core_ref: (plan_ref[core_ref[0], c], 0, 0))
    return pl.pallas_call(
        functools.partial(cross_kernel, scale),
        grid_spec=pltpu.PrefetchScalarGridSpec(
            num_scalar_prefetch=2,
            grid=(blocks,),
            in_specs=[own, own, mate, mate],
            out_specs=pl.BlockSpec((1, 2, channels, channels), lambda c, plan_ref, core_ref: (c, 0, 0, 0)),
        ),
        out_shape=jax.ShapeDtypeStruct((blocks, 2, channels, channels), jnp.bfloat16),
        compiler_params=pltpu.CompilerParams(vmem_limit_bytes=VMEM),
        name="cross",
    )(plan, core, here, other, here, other)


def join_kernel(core_ref, mine_ref, other_ref, out_ref):
    core = core_ref[0]
    mine = mine_ref[0].astype(jnp.float32)
    other = other_ref[0].astype(jnp.float32)
    out_ref[0, core] = mine
    out_ref[0, 1 - core] = other


def join(core, mine, other):
    bins, halves, rows, channels = other.shape
    return pl.pallas_call(
        join_kernel,
        grid_spec=pltpu.PrefetchScalarGridSpec(
            num_scalar_prefetch=1,
            grid=(bins,),
            in_specs=[
                pl.BlockSpec((1, halves, rows, channels), lambda i, core_ref: (bins * core_ref[0] + i, 0, 0, 0)),
                pl.BlockSpec((1, halves, rows, channels), lambda i, core_ref: (i, 0, 0, 0)),
            ],
            out_specs=pl.BlockSpec((1, ROUNDS, halves, rows, channels), lambda i, core_ref: (i, 0, 0, 0, 0)),
        ),
        out_shape=jax.ShapeDtypeStruct((bins, ROUNDS, halves, rows, channels), jnp.float32),
        compiler_params=pltpu.CompilerParams(vmem_limit_bytes=VMEM),
        name="join",
    )(core, mine, other)


def on_device(dft, records, fir_taps, plan):
    channels, samples_here = records.shape
    chips = lax.axis_size("chip")
    cores = lax.axis_size("core")
    blocks = lax.axis_size("chan")
    core = lax.axis_index("core").astype(jnp.int32)
    count = chips * cores
    tail = lax.ppermute(
        records[:, samples_here - WL // 2 :], ("chip", "core"), [(i, i + 1) for i in range(count - 1)]
    )
    swap = [(0, 1), (1, 0)]
    scale = 1.0 / math.sqrt(samples_here // WL * count)
    white = spectra(tail, make_table(fir_taps, dft), records)
    here = lax.all_to_all(white, ("chan", "chip"), 0, 0, tiled=True)
    here = here.reshape(blocks, chips * ROWS, channels)
    other = lax.ppermute(here, "core", swap)
    core = core.reshape(1)
    products = cross(plan, core, here, other, scale)
    mine = lax.all_to_all(products, "chan", 0, 0, tiled=True)
    bins = blocks // cores
    away = lax.dynamic_slice_in_dim(mine, bins * (1 - core[0]), bins, 0)
    return join(core, mine, lax.ppermute(away, "core", swap))


def solution(mesh):
    blocks, count = mesh.devices.shape
    chips = count // 2
    inner = Mesh(mesh.devices.reshape(blocks, chips, 2), ("chan", "chip", "core"))
    dft = dft_rows(chips, blocks)

    def step(records, fir_taps, plan):
        return jax.shard_map(
            on_device,
            mesh=inner,
            in_specs=(P(), P("chan", ("chip", "core")), P(), P()),
            out_specs=P(("chip", "core"), None, None, None, "chan"),
            check_vma=False,
        )(jnp.asarray(dft), records, fir_taps, plan)

    return step
```

time: 1220 us -> 117 us (0.10)
  waiting for transfers between devices: 677 us -> 35.1 us
  local copies, waits for them, and re-layouts: 469 us -> 3.79 us
  blocking collectives: 0 us -> 44.7 us
  matrix products: 27.2 us -> 0 us
  Pallas kernels: 0 us -> 21.1 us
  between operations: 15 us -> 0.09 us
  other arithmetic: 14.1 us -> 0 us
    gather x2 -> x0, local copies, waits for them, and re-layouts: 454 us -> none  [fir_matrix(): picked = fir_taps[jnp.clip(tap_number, 0, TAPS - 1)]]
    reduce_scatter x1 -> x0, waiting for transfers between devices: 349 us -> none  [on_device(): lax.psum_scatter(cross_term(partner_rows, whitened, scale).astype(jnp.bfl...]
    ppermute x8 -> x3, waiting for transfers between devices: 329 us -> 6.96 us  [the longest x1 4.67 us: on_device(): other = lax.ppermute(here, 'core', swap)]
    all_to_all x0 -> x1, blocking collectives: none -> 44.7 us  [on_device(): here = lax.all_to_all(white, ('chan', 'chip'), 0, 0, tiled=True)]
    all_to_all x0 -> x1, waiting for transfers between devices: none -> 28.1 us  [on_device(): mine = lax.all_to_all(products, 'chan', 0, 0, tiled=True)]
    dot_general x4 -> x0, matrix products: 27.2 us -> none  [the longest x1 18.2 us: cross_term(): lax.dot_general(partner_piece, own_piece, (((1, 2), (1, 2)), ((0,), (0,))...]
    pallas_call x0 -> x4, Pallas kernels: none -> 21.1 us  [the longest x1 9.85 us: spectra(): pl.pallas_call(spectra_kernel, grid=(steps,), out_shape=jax.ShapeDtypeStr...]
  transfers between devices with their start and end apart: 9 -> 4, of which waited for: 6 -> 3; matrix products, arithmetic and copies ran while one was open for 38% -> 0% of each run, Pallas kernels for 0% -> 1%
where the time goes in v1:
time: 117 us
  blocking collectives  44.7 us (38%)
  waiting for transfers between devices  35.1 us (30%)
  Pallas kernels  21.1 us (18%)
  starting transfers between devices  12.1 us (10%)
  local copies, waits for them, and re-layouts  3.79 us (3%)
    all_to_all x1, blocking collectives, on_device(): here = lax.all_to_all(white, ('chan', 'chip'), 0, 0, tiled=True)  44.7 us
    all_to_all x1, waiting for transfers between devices, on_device(): mine = lax.all_to_all(products, 'chan', 0, 0, tiled=True)  28.1 us
    pallas_call x1, Pallas kernels, spectra(): pl.pallas_call(spectra_kernel, grid=(steps,), out_shape=jax.ShapeDtypeStr...  9.85 us
    pallas_call x1, Pallas kernels, cross(): pl.pallas_call(functools.partial(cross_kernel, scale), grid_spec=pltpu.Pr...  7.79 us
    ppermute x1, waiting for transfers between devices, on_device(): other = lax.ppermute(here, 'core', swap)  4.67 us
    ppermute x1, starting transfers between devices, on_device(): lax.ppermute(records[:, samples_here - WL // 2:], ('chip', 'core'), [(i,...  4.58 us
    all_to_all x1, starting transfers between devices, on_device(): mine = lax.all_to_all(products, 'chan', 0, 0, tiled=True)  3.6 us
    unnamed x8, local copies, waits for them, and re-layouts  2.87 us
  transfers between devices with their start and end apart: 4, of which 3 were waited for; matrix products, arithmetic and copies ran while one was open for 0% of the time, Pallas kernels for 1%

profile of v1, /device:TPU:1, one launch (start us, length us, event | category | flops | bytes accessed | tf_op | source)
XLA Modules:
  0.0 116.9 jit_solution(4858021128535136780)
XLA Ops:
  0.0 0.8 slice.3
  0.8 4.6 %collective-permute-start = (bf16[256,128]{1,0:T(8,128)(2,1)S(1)}, bf16[256,128]{1,0:T(8,128)(2,1)S(1)}, u32[]{:S(2)}, u32[]{:S(2)}) collective-permute-start(bf16[256,128]{1,0:T(8,128)(2,1)S(1)} %slice.3), channel_id=1, source_target_pairs={{0,1},{1,2},{2,3},{3,4},{4,5},{5,6},{6,7},{7,8},{8,9},{9,10},{10,1... | collective-permute-start | bytes 196616 | tf_op jit(solution)/shard_map/ppermute | solution.py:218
  5.4 0.0 copy-start.1
  5.4 0.9 copy-done.1
  6.3 0.0 copy-start.3
  6.3 0.7 copy-done.3
  7.0 1.1 table.1.table_ref
  8.1 0.0 collective-permute-done.tail_ref
  8.1 9.8 %spectra.1 = bf16[64,80,256]{2,1,0:T(8,128)(2,1)S(1)} custom-call(bf16[256,128]{1,0:T(8,128)(2,1)S(1)} %collective-permute-done.tail_ref, bf16[768,256]{1,0:T(8,128)(2,1)S(1)} %table.1.table_ref, bf16[256,10240]{1,0:T(8,128)(2,1)} %records_ref.1), custom_call_target="tpu_custom_call" | custom-call | tf_op jit(solution)/shard_map/spectra/pallas_call | solution.py:120
  17.9 0.0 copy-start.2
  17.9 44.7 %all_to_all.10 = bf16[64,80,256]{2,1,0:T(8,128)(2,1)S(1)} all-to-all(bf16[64,80,256]{2,1,0:T(8,128)(2,1)S(1)} %spectra.1), channel_id=1, replica_groups=mesh['chan'=8,'chip'=8,'core'=2] {'chan','chip'}, dimensions={0} | all-to-all | bytes 5242880 | tf_op jit(solution)/shard_map/all_to_all | solution.py:224
  62.7 2.6 %collective-permute-start.1 = (bf16[8,640,256]{2,1,0:T(8,128)(2,1)S(1)}, bf16[8,640,256]{2,1,0:T(8,128)(2,1)}, u32[]{:S(2)}, u32[]{:S(2)}) collective-permute-start(bf16[8,640,256]{2,1,0:T(8,128)(2,1)S(1)} %bitcast.2), channel_id=1, source_target_pairs={{0,1},{1,0},{2,3},{3,2},{4,5},{5,4},{6,7},{7,6},{8,9},{9,8},{10,11... | collective-permute-start | bytes 7864328 | tf_op jit(solution)/shard_map/ppermute | solution.py:226
  65.3 4.7 %collective-permute-done.1.own_other_ref.mate_other_ref = bf16[8,640,256]{2,1,0:T(8,128)(2,1)} collective-permute-done((bf16[8,640,256]{2,1,0:T(8,128)(2,1)S(1)}, bf16[8,640,256]{2,1,0:T(8,128)(2,1)}, u32[]{:S(2)}, u32[]{:S(2)}) %collective-permute-start.1) | collective-permute-done | bytes 2621472 | tf_op jit(solution)/shard_map/ppermute | solution.py:226
  69.9 0.0 copy-done.2
  69.9 7.8 %cross.1 = bf16[8,2,256,256]{3,2,1,0:T(8,128)(2,1)S(1)} custom-call(s32[2,8]{1,0:T(2,128)S(1)} %copy-done.2, s32[1]{0:T(128)} %bitcast.core_ref, bf16[8,640,256]{2,1,0:T(8,128)(2,1)S(1)} %bitcast.3, bf16[8,640,256]{2,1,0:T(8,128)(2,1)} %collective-permute-done.1.own_other_ref.mate_other_ref, bf16[8,640,256]{2,1,0:T(8,128)(2,1)S(1)} %bitcast.4, ...), custom_call_target="tpu_custom_call" | custom-call | tf_op jit(solution)/shard_map/cross/pallas_call | solution.py:170
  77.7 0.0 copy-start
  77.8 1.3 %copy-done = bf16[8,2,256,256]{3,2,1,0:T(8,128)(2,1)} copy-done((bf16[8,2,256,256]{3,2,1,0:T(8,128)(2,1)}, bf16[8,2,256,256]{3,2,1,0:T(8,128)(2,1)S(1)}, u32[]{:S(2)}) %copy-start) | copy-done | bytes 2097176
  79.1 3.6 %all-to-all-start.1 = ((bf16[8,2,256,256]{3,2,1,0:T(8,128)(2,1)}), bf16[8,2,256,256]{3,2,1,0:T(8,128)(2,1)S(1)}, u32[]{:S(2)}, u32[]{:S(2)}) async-start(bf16[8,2,256,256]{3,2,1,0:T(8,128)(2,1)} %copy-done), calls=%async_computation.1 | async-start | bytes 4194304 | tf_op jit(solution)/shard_map/all_to_all | solution.py:229
  82.7 28.1 %all-to-all-done.1.mine_ref = bf16[8,2,256,256]{3,2,1,0:T(8,128)(2,1)S(1)} async-done(((bf16[8,2,256,256]{3,2,1,0:T(8,128)(2,1)}), bf16[8,2,256,256]{3,2,1,0:T(8,128)(2,1)S(1)}, u32[]{:S(2)}, u32[]{:S(2)}) %all-to-all-start.1) | async-done | bytes 2097184 | tf_op jit(solution)/shard_map/all_to_all | solution.py:229
  110.8 0.1 constant_dynamic-slice_fusion
  110.9 1.3 %collective-permute-start.2 = (bf16[4,2,256,256]{3,2,1,0:T(8,128)(2,1)S(1)}, bf16[4,2,256,256]{3,2,1,0:T(8,128)(2,1)S(1)}, u32[]{:S(2)}, u32[]{:S(2)}) collective-permute-start(bf16[4,2,256,256]{3,2,1,0:T(8,128)(2,1)S(1)} %constant_dynamic-slice_fusion), channel_id=1, source_target_pairs={{0,1},{1,0},{2,3},{3,2},{4,5},{5,4},{6,7},{7,6},{8,9},{9,8},{10,11... | collective-permute-start | bytes 3145736 | tf_op jit(solution)/shard_map/ppermute | solution.py:232
  112.2 2.3 %collective-permute-done.2.other_ref = bf16[4,2,256,256]{3,2,1,0:T(8,128)(2,1)S(1)} collective-permute-done((bf16[4,2,256,256]{3,2,1,0:T(8,128)(2,1)S(1)}, bf16[4,2,256,256]{3,2,1,0:T(8,128)(2,1)S(1)}, u32[]{:S(2)}, u32[]{:S(2)}) %collective-permute-start.2) | collective-permute-done | bytes 1048608 | tf_op jit(solution)/shard_map/ppermute | solution.py:232
  114.5 2.4 %join.1 = f32[4,2,2,256,256]{4,3,2,1,0:T(8,128)} custom-call(s32[1]{0:T(128)} %bitcast.core_ref, bf16[8,2,256,256]{3,2,1,0:T(8,128)(2,1)S(1)} %all-to-all-done.1.mine_ref, bf16[4,2,256,256]{3,2,1,0:T(8,128)(2,1)S(1)} %collective-permute-done.2.other_ref), custom_call_target="tpu_custom_call" | custom-call | tf_op jit(solution)/shard_map/join/pallas_call | solution.py:194
Async XLA Ops:
  0.8 7.2 %collective-permute-start = (bf16[256,128]{1,0:T(8,128)(2,1)S(1)}, bf16[256,128]{1,0:T(8,128)(2,1)S(1)}, u32[]{:S(2)}, u32[]{:S(2)}) collective-permute-start(bf16[256,128]{1,0:T(8,128)(2,1)S(1)} %slice.3), channel_id=1, source_target_pairs={{0,1},{1,2},{2,3},{3,4},{4,5},{5,6},{6,7},{7,8},{8,9},{9,10},{10,1... | collective-permute-start | bytes 196616 | tf_op jit(solution)/shard_map/ppermute | solution.py:218
  5.4 0.9 copy-start.1
  6.3 0.7 copy-start.3
  17.9 52.0 %copy-start.2 = (s32[2,8]{1,0:T(2,128)S(1)}, s32[2,8]{1,0:T(2,128)}, u32[]{:S(2)}) copy-start(s32[2,8]{1,0:T(2,128)} %plan_ref.1) | copy-start | bytes 196
  62.7 7.3 %collective-permute-start.1 = (bf16[8,640,256]{2,1,0:T(8,128)(2,1)S(1)}, bf16[8,640,256]{2,1,0:T(8,128)(2,1)}, u32[]{:S(2)}, u32[]{:S(2)}) collective-permute-start(bf16[8,640,256]{2,1,0:T(8,128)(2,1)S(1)} %bitcast.2), channel_id=1, source_target_pairs={{0,1},{1,0},{2,3},{3,2},{4,5},{5,4},{6,7},{7,6},{8,9},{9,8},{10,11... | collective-permute-start | bytes 7864328 | tf_op jit(solution)/shard_map/ppermute | solution.py:226
  77.7 1.3 %copy-start = (bf16[8,2,256,256]{3,2,1,0:T(8,128)(2,1)}, bf16[8,2,256,256]{3,2,1,0:T(8,128)(2,1)S(1)}, u32[]{:S(2)}) copy-start(bf16[8,2,256,256]{3,2,1,0:T(8,128)(2,1)S(1)} %cross.1) | copy-start | bytes 6291460
  79.1 31.7 %all-to-all-start.1 = ((bf16[8,2,256,256]{3,2,1,0:T(8,128)(2,1)}), bf16[8,2,256,256]{3,2,1,0:T(8,128)(2,1)S(1)}, u32[]{:S(2)}, u32[]{:S(2)}) async-start(bf16[8,2,256,256]{3,2,1,0:T(8,128)(2,1)} %copy-done), calls=%async_computation.1 | async-start | bytes 4194304 | tf_op jit(solution)/shard_map/all_to_all | solution.py:229
  110.9 3.6 %collective-permute-start.2 = (bf16[4,2,256,256]{3,2,1,0:T(8,128)(2,1)S(1)}, bf16[4,2,256,256]{3,2,1,0:T(8,128)(2,1)S(1)}, u32[]{:S(2)}, u32[]{:S(2)}) collective-permute-start(bf16[4,2,256,256]{3,2,1,0:T(8,128)(2,1)S(1)} %constant_dynamic-slice_fusion), channel_id=1, source_target_pairs={{0,1},{1,0},{2,3},{3,2},{4,5},{5,4},{6,7},{7,6},{8,9},{9,8},{10,11... | collective-permute-start | bytes 3145736 | tf_op jit(solution)/shard_map/ppermute | solution.py:232

commit v2 on v1

v2 whole, which is shorter than its diff:
```python
import functools
import math

import jax
import jax.numpy as jnp
import numpy as np
from jax import lax
from jax.experimental import pallas as pl
from jax.experimental.pallas import tpu as pltpu
from jax.sharding import Mesh
from jax.sharding import PartitionSpec as P

WL = 256
F = 64
TAPS = 64
ROUNDS = 2
STEP_WINDOWS = 8
PIECES = 3
TILE = 16
VMEM = 50 * 1024 * 1024
SMALL_VMEM = 8 * 1024 * 1024
CALLS = ((2, 4, 6, 5), (3, 0, 7, 1))


def dft_rows(chips, blocks):
    place = np.arange(F)
    bin_number = blocks * (place % chips) + place // chips + 1
    phase = np.arange(WL)[None, :] * bin_number[:, None] % WL * (2.0 * math.pi / WL)
    return np.concatenate([np.cos(phase), -np.sin(phase)]).astype(np.float32)


def in_pieces(table):
    pieces = []
    rest = table
    for _ in range(PIECES):
        piece = rest.astype(jnp.bfloat16).astype(jnp.float32)
        pieces.append(piece)
        rest = rest - piece
    return pieces


def table_kernel(taps_ref, dft_ref, main_ref, before_ref, order_ref):
    lane = lax.broadcasted_iota(jnp.int32, (1, 2 * WL), 1)
    reversed_taps = jnp.zeros((1, 2 * WL), jnp.float32)
    for tap in range(TAPS):
        reversed_taps = jnp.where(lane == TAPS - 1 - tap, taps_ref[tap], reversed_taps)
    spread = jnp.broadcast_to(reversed_taps, (WL, 2 * WL))
    toeplitz = pltpu.roll(spread, WL - TAPS + 1, 1, stride=1, stride_axis=0)
    combined = jnp.dot(
        dft_ref[...], toeplitz, precision=lax.Precision.HIGHEST, preferred_element_type=jnp.float32
    )
    main_ref[...] = jnp.concatenate(in_pieces(combined[:, WL:]), axis=0).astype(jnp.bfloat16)
    high, middle, low = in_pieces(combined[:, WL // 2 : WL])
    left = lax.broadcasted_iota(jnp.int32, high.shape, 1) < TAPS
    first = jnp.where(left, pltpu.roll(high, TAPS, 1), middle)
    second = jnp.where(left, pltpu.roll(low, TAPS, 1), 0.0)
    before_ref[...] = jnp.concatenate([first, second], axis=1).astype(jnp.bfloat16)
    row = lax.broadcasted_iota(jnp.int32, order_ref.shape, 0)
    column = lax.broadcasted_iota(jnp.int32, order_ref.shape, 1)
    source = (row & 7) * 32 + ((row >> 3) & 1) * 16 + (row >> 4)
    order_ref[...] = jnp.where(column == source, 1.0, 0.0).astype(jnp.bfloat16)


IN_VMEM = pl.BlockSpec(memory_space=pltpu.VMEM)
IN_SMEM = pl.BlockSpec(memory_space=pltpu.SMEM)
IN_HBM = pl.BlockSpec(memory_space=pltpu.HBM)


def make_tables(fir_taps, dft):
    rows = (PIECES * 2 * F, 2 * F, WL)
    return pl.pallas_call(
        table_kernel,
        out_shape=[jax.ShapeDtypeStruct((count, WL), jnp.bfloat16) for count in rows],
        in_specs=[IN_SMEM, IN_VMEM],
        out_specs=[IN_VMEM] * 3,
        compiler_params=pltpu.CompilerParams(vmem_limit_bytes=SMALL_VMEM),
        name="table",
    )(fir_taps, dft)


NT = (((1,), (1,)), ((), ()))


def last_samples(samples):
    end = samples[:, samples.shape[1] - TAPS :]
    return jnp.concatenate([end] * (WL // TAPS), axis=1)


def spectra_kernel(
    tail_ref, main_ref, before_ref, order_ref, records_ref, out_ref, samples_ref, carry_ref, held_ref, sems
):
    groups = samples_ref.shape[0]
    width = STEP_WINDOWS * WL
    count = 2 * F

    def fetch(group):
        source = records_ref.at[:, pl.ds(pl.multiple_of(group * width, width), width)]
        return pltpu.make_async_copy(source, samples_ref.at[group], sems.at[group])

    for group in range(groups):
        fetch(group).start()
    before = before_ref[...]
    carry_ref[...] = lax.dot_general(
        before, last_samples(tail_ref[...]), NT, preferred_element_type=jnp.float32
    )

    @pl.loop(0, groups)
    def _(group):
        fetch(group).wait()
        carry = carry_ref[...]
        for inner in range(STEP_WINDOWS):
            samples = samples_ref[group, :, inner * WL : (inner + 1) * WL]
            rows = lax.dot_general(main_ref[...], samples, NT, preferred_element_type=jnp.float32)
            stacked = rows[2 * count :] + rows[count : 2 * count] + carry + rows[:count]
            carry = lax.dot_general(
                before, last_samples(samples), NT, preferred_element_type=jnp.float32
            )
            power = jnp.sum(stacked * stacked, axis=0, keepdims=True) * (1.0 / count) + 1e-06
            held_ref[inner] = (stacked * (1.0 / jnp.sqrt(power))).astype(jnp.bfloat16)
        carry_ref[...] = carry
        for part in range(F // TILE):
            rows = []
            for inner in range(STEP_WINDOWS):
                for start in (part * TILE, F + part * TILE):
                    rows.append(held_ref[inner, start : start + TILE, :])
            placed = jnp.dot(
                order_ref[...], jnp.concatenate(rows, axis=0), preferred_element_type=jnp.float32
            ).astype(jnp.bfloat16)
            at = pl.ds(pl.multiple_of(group * TILE, TILE), TILE)
            for n in range(TILE):
                out_ref[part * TILE + n, at, :] = placed[n * TILE : (n + 1) * TILE]


def spectra(tail, tables, records):
    channels, samples = records.shape
    groups = samples // WL // STEP_WINDOWS
    return pl.pallas_call(
        spectra_kernel,
        out_shape=jax.ShapeDtypeStruct((F, groups * TILE, channels), jnp.bfloat16),
        in_specs=[IN_VMEM] * 4 + [IN_HBM],
        out_specs=IN_VMEM,
        scratch_shapes=[
            pltpu.VMEM((groups, channels, STEP_WINDOWS * WL), jnp.bfloat16),
            pltpu.VMEM((2 * F, channels), jnp.float32),
            pltpu.VMEM((STEP_WINDOWS, 2 * F, channels), jnp.bfloat16),
            pltpu.SemaphoreType.DMA((groups,)),
        ],
        compiler_params=pltpu.CompilerParams(vmem_limit_bytes=VMEM),
        name="spectra",
    )(tail, *tables, records)


def rotated(rows):
    wide = rows.astype(jnp.float32)
    layers = []
    for start in range(0, rows.shape[0], TILE):
        middle = start + TILE // 2
        layers += [wide[middle : start + TILE], -wide[start:middle]]
    return jnp.concatenate(layers, axis=0).astype(jnp.bfloat16)


TN = (((0,), (0,)), ((), ()))


def target(step, half, place, core):
    return place ^ (step // 2) ^ (half * ((step % 2) ^ core))


def cross_kernel(scale, steps, plan_ref, place_ref, here_ref, other_ref, *out_refs):
    half_blocks = here_ref.shape[0] // 2
    for step, out_ref in zip(steps, out_refs):
        own_at = target(step, half_blocks, place_ref[0], place_ref[1])
        mate_at = plan_ref[place_ref[1], own_at]
        own = jnp.concatenate([here_ref[own_at], other_ref[own_at]], axis=0)
        mate = jnp.concatenate([here_ref[mate_at], other_ref[mate_at]], axis=0)
        for half, rows in enumerate((own, rotated(own))):
            product = lax.dot_general(mate, rows, TN, preferred_element_type=jnp.float32) * scale
            out_ref[half] = product.astype(jnp.bfloat16)


def cross(steps, plan, place, here, other, scale):
    depth, channels = here.shape[1:]
    return pl.pallas_call(
        functools.partial(cross_kernel, scale, steps),
        in_specs=[IN_SMEM, IN_SMEM, IN_VMEM, IN_VMEM],
        out_specs=[IN_VMEM] * len(steps),
        out_shape=[jax.ShapeDtypeStruct((2, channels, channels), jnp.bfloat16)] * len(steps),
        compiler_params=pltpu.CompilerParams(vmem_limit_bytes=SMALL_VMEM),
        cost_estimate=pl.CostEstimate(
            flops=len(steps) * 2 * 2 * 2 * depth * channels * channels,
            bytes_accessed=len(steps) * (8 * depth * channels + 4 * channels * channels),
            transcendentals=0,
        ),
        name="cross",
    )(plan, place, here, other)


def join_kernel(steps, bins, place_ref, *refs):
    parts, (out_ref, wide_ref, sems) = refs[:-3], refs[-3:]
    copies = []
    for n, step in enumerate(steps):
        own_bin = (place_ref[0] % bins) ^ (step // 2)
        round_index = (place_ref[0] // bins) ^ place_ref[1] ^ (step % 2)
        wide_ref[n] = parts[n][...].astype(jnp.float32)
        copy = pltpu.make_async_copy(wide_ref.at[n], out_ref.at[own_bin, round_index], sems.at[n])
        copy.start()
        copies.append(copy)
    for copy in copies:
        copy.wait()


def join(steps, place, parts, bins):
    halves, rows, channels = parts[0].shape
    return pl.pallas_call(
        functools.partial(join_kernel, steps, bins),
        in_specs=[IN_SMEM] + [IN_VMEM] * len(steps),
        out_specs=pl.BlockSpec(memory_space=pl.ANY),
        out_shape=jax.ShapeDtypeStruct((bins, ROUNDS, halves, rows, channels), jnp.float32),
        scratch_shapes=[
            pltpu.VMEM((len(steps), halves, rows, channels), jnp.float32),
            pltpu.SemaphoreType.DMA((len(steps),)),
        ],
        compiler_params=pltpu.CompilerParams(vmem_limit_bytes=SMALL_VMEM),
        name="join",
    )(place, *parts)


def on_device(dft, records, fir_taps, plan):
    channels, samples_here = records.shape
    chips = lax.axis_size("chip")
    cores = lax.axis_size("core")
    blocks = lax.axis_size("chan")
    core = lax.axis_index("core").astype(jnp.int32)
    count = chips * cores
    tail = lax.ppermute(
        records[:, samples_here - WL // 2 :], ("chip", "core"), [(i, i + 1) for i in range(count - 1)]
    )
    swap = [(0, 1), (1, 0)]
    scale = 1.0 / math.sqrt(samples_here // WL * count)
    white = spectra(tail, make_tables(fir_taps, dft), records)
    here = lax.all_to_all(white, ("chan", "chip"), 0, 0, tiled=True)
    here = here.reshape(blocks, chips * white.shape[1], channels)
    other = lax.ppermute(here, "core", swap)
    half = blocks // 2
    place = jnp.stack([lax.axis_index("chan").astype(jnp.int32), core])
    steps = [step for call in CALLS for step in call]
    parts = []
    for call in CALLS:
        products = cross(call, plan, place, here, other, scale)
        here, other, *products = lax.optimization_barrier((here, other, *products))
        for step, product in zip(call, products):
            route = [
                (j * cores + h, target(step, half, j, h) * cores + j // half)
                for j in range(blocks)
                for h in range(cores)
            ]
            parts.append(lax.ppermute(product, ("chan", "core"), route))
    return join(steps, place, parts, half)


def solution(mesh):
    blocks, count = mesh.devices.shape
    chips = count // 2
    inner = Mesh(mesh.devices.reshape(blocks, chips, 2), ("chan", "chip", "core"))
    dft = dft_rows(chips, blocks)

    def step(records, fir_taps, plan):
        return jax.shard_map(
            on_device,
            mesh=inner,
            in_specs=(P(), P("chan", ("chip", "core")), P(), P()),
            out_specs=P(("chip", "core"), None, None, None, "chan"),
            check_vma=False,
        )(jnp.asarray(dft), records, fir_taps, plan)

    return step
```

time: 117 us -> 103 us (0.88)
  waiting for transfers between devices: 35.1 us -> 13.1 us
  starting transfers between devices: 12.1 us -> 23.8 us
  Pallas kernels: 21.1 us -> 18 us
  local copies, waits for them, and re-layouts: 3.79 us -> 2.4 us
    all_to_all x1 -> x0, waiting for transfers between devices: 28.1 us -> none  [on_device(): mine = lax.all_to_all(products, 'chan', 0, 0, tiled=True)]
    ppermute x1 -> x8, starting transfers between devices: 1.33 us -> 16.8 us  [on_device(): parts.append(lax.ppermute(product, ('chan', 'core'), route))]
    ppermute x1 -> x8, waiting for transfers between devices: 2.29 us -> 8.49 us  [on_device(): parts.append(lax.ppermute(product, ('chan', 'core'), route))]
    all_to_all x1 -> x0, starting transfers between devices: 3.6 us -> none  [on_device(): mine = lax.all_to_all(products, 'chan', 0, 0, tiled=True)]
    pallas_call x4 -> x5, Pallas kernels: 21.1 us -> 18 us  [the longest x1 7.59 us: spectra(): pl.pallas_call(spectra_kernel, out_shape=jax.ShapeDtypeStruct((F, groups...]
    unnamed x8 -> x6, local copies, waits for them, and re-layouts: 2.87 us -> 1.56 us
  transfers between devices with their start and end apart: 4 -> 10, of which waited for: 3 -> 6; matrix products, arithmetic and copies ran while one was open for 0% -> 0% of each run, Pallas kernels for 1% -> 4%
where the time goes in v2:
time: 103 us; the launch traced here: 102 us
  blocking collectives  44.9 us (44%)
  starting transfers between devices  23.8 us (23%)
  Pallas kernels  18 us (17%)
  waiting for transfers between devices  13.1 us (13%)
  local copies, waits for them, and re-layouts  2.4 us (2%)
    all_to_all x1, blocking collectives, on_device(): here = lax.all_to_all(white, ('chan', 'chip'), 0, 0, tiled=True)  44.9 us
    ppermute x8, starting transfers between devices, on_device(): parts.append(lax.ppermute(product, ('chan', 'core'), route))  16.8 us
    ppermute x8, waiting for transfers between devices, on_device(): parts.append(lax.ppermute(product, ('chan', 'core'), route))  8.49 us
    pallas_call x1, Pallas kernels, spectra(): pl.pallas_call(spectra_kernel, out_shape=jax.ShapeDtypeStruct((F, groups...  7.59 us
    pallas_call x2, Pallas kernels, cross(): pl.pallas_call(functools.partial(cross_kernel, scale, steps), in_specs=[I...  6.6 us
    ppermute x1, waiting for transfers between devices, on_device(): other = lax.ppermute(here, 'core', swap)  4.59 us
    ppermute x1, starting transfers between devices, on_device(): lax.ppermute(records[:, samples_here - WL // 2:], ('chip', 'core'), [(i,...  4.58 us
    pallas_call x1, Pallas kernels, join(): pl.pallas_call(functools.partial(join_kernel, steps, bins), in_specs=[IN_...  2.64 us
  transfers between devices with their start and end apart: 10, of which 6 were waited for; matrix products, arithmetic and copies ran while one was open for 0% of the time, Pallas kernels for 4%

profile of v2, /device:TPU:1, one launch (start us, length us, event | category | flops | bytes accessed | tf_op | source)
XLA Modules:
  0.0 102.4 jit_solution(16748296718933580042)
XLA Ops:
  0.0 0.8 slice.3
  0.8 4.6 %collective-permute-start = (bf16[256,128]{1,0:T(8,128)(2,1)S(1)}, bf16[256,128]{1,0:T(8,128)(2,1)S(1)}, u32[]{:S(2)}, u32[]{:S(2)}) collective-permute-start(bf16[256,128]{1,0:T(8,128)(2,1)S(1)} %slice.3), channel_id=1, source_target_pairs={{0,1},{1,2},{2,3},{3,4},{4,5},{5,6},{6,7},{7,8},{8,9},{9,10},{10,1... | collective-permute-start | bytes 196616 | tf_op jit(solution)/shard_map/ppermute | solution.py:235
  5.4 0.9 copy-done
  6.3 0.7 copy-done.2
  7.0 1.1 %table.1 = (bf16[384,256]{1,0:T(8,128)(2,1)S(1)}, bf16[128,256]{1,0:T(8,128)(2,1)S(1)}, bf16[256,256]{1,0:T(8,128)(2,1)S(1)}) custom-call(f32[64]{0:T(128)S(1)} %copy-done.2, f32[128,256]{1,0:T(8,128)S(1)} %copy-done), custom_call_target="tpu_custom_call" | custom-call | tf_op jit(solution)/shard_map/table/pallas_call | solution.py:71
  8.2 7.6 %spectra.1 = bf16[64,80,256]{2,1,0:T(8,128)(2,1)S(1)} custom-call(bf16[256,128]{1,0:T(8,128)(2,1)S(1)} %collective-permute-done.tail_ref, bf16[384,256]{1,0:T(8,128)(2,1)S(1)} %get-tuple-element.26.main_ref, bf16[128,256]{1,0:T(8,128)(2,1)S(1)} %get-tuple-element.27.before_ref, bf16[256,256]{1,0:T(8,128)(2,1)S(1)} %get-tuple-element.28.order_ref, ...), custom_call_target="tpu_custom_call" | custom-call | tf_op jit(solution)/shard_map/spectra/pallas_call | solution.py:137
  15.8 44.9 %all_to_all.5 = bf16[64,80,256]{2,1,0:T(8,128)(2,1)S(1)} all-to-all(bf16[64,80,256]{2,1,0:T(8,128)(2,1)S(1)} %spectra.1), channel_id=1, replica_groups=mesh['chan'=8,'chip'=8,'core'=2] {'chan','chip'}, dimensions={0} | all-to-all | bytes 5242880 | tf_op jit(solution)/shard_map/all_to_all | solution.py:241
  60.7 2.4 %collective-permute-start.1 = (bf16[8,640,256]{2,1,0:T(8,128)(2,1)S(1)}, bf16[8,640,256]{2,1,0:T(8,128)(2,1)}, u32[]{:S(2)}, u32[]{:S(2)}) collective-permute-start(bf16[8,640,256]{2,1,0:T(8,128)(2,1)S(1)} %bitcast.3), channel_id=1, source_target_pairs={{0,1},{1,0},{2,3},{3,2},{4,5},{5,4},{6,7},{7,6},{8,9},{9,8},{10,11... | collective-permute-start | bytes 7864328 | tf_op jit(solution)/shard_map/ppermute | solution.py:243
  63.1 0.1 pad_add_fusion.place_ref
  63.2 4.6 %collective-permute-done.1.other_ref = bf16[8,640,256]{2,1,0:T(8,128)(2,1)} collective-permute-done((bf16[8,640,256]{2,1,0:T(8,128)(2,1)S(1)}, bf16[8,640,256]{2,1,0:T(8,128)(2,1)}, u32[]{:S(2)}, u32[]{:S(2)}) %collective-permute-start.1) | collective-permute-done | bytes 2621472 | tf_op jit(solution)/shard_map/ppermute | solution.py:243
  67.8 3.3 %cross.2 = (bf16[2,256,256]{2,1,0:T(8,128)(2,1)S(1)}, bf16[2,256,256]{2,1,0:T(8,128)(2,1)S(1)}, bf16[2,256,256]{2,1,0:T(8,128)(2,1)S(1)}, bf16[2,256,256]{2,1,0:T(8,128)(2,1)S(1)}) custom-call(s32[2,8]{1,0:T(2,128)S(1)} %copy-done.1, s32[2]{0:T(128)S(1)} %pad_add_fusion.place_ref, bf16[8,640,256]{2,1,0:T(8,128)(2,1)S(1)} %bitcast.4, ...), custom_call_target="tpu_custom_call" | custom-call | flops 1342177280 | bytes 6291456 | tf_op jit(solution)/shard_map/cross/pallas_call | solution.py:183
  71.1 2.0 %collective-permute-start.2 = (bf16[2,256,256]{2,1,0:T(8,128)(2,1)S(1)}, bf16[2,256,256]{2,1,0:T(8,128)(2,1)S(1)}, u32[]{:S(2)}, u32[]{:S(2)}) collective-permute-start(bf16[2,256,256]{2,1,0:T(8,128)(2,1)S(1)} %get-tuple-element.33), channel_id=1, source_target_pairs={{0,16},{1,80},{16,0},{17,64},{32,48},{33,112},{48,32},{49,96},{64,... | collective-permute-start | bytes 786440 | tf_op jit(solution)/shard_map/ppermute | solution.py:257
  73.1 4.0 %collective-permute-start.4 = (bf16[2,256,256]{2,1,0:T(8,128)(2,1)S(1)}, bf16[2,256,256]{2,1,0:T(8,128)(2,1)S(1)}, u32[]{:S(2)}, u32[]{:S(2)}) collective-permute-start(bf16[2,256,256]{2,1,0:T(8,128)(2,1)S(1)} %get-tuple-element.35), channel_id=1, source_target_pairs={{0,48},{1,112},{16,32},{17,96},{32,16},{33,80},{48,0},{49,64},{64,... | collective-permute-start | bytes 786440 | tf_op jit(solution)/shard_map/ppermute | solution.py:257
  77.1 3.3 %cross.3 = (bf16[2,256,256]{2,1,0:T(8,128)(2,1)S(1)}, bf16[2,256,256]{2,1,0:T(8,128)(2,1)S(1)}, bf16[2,256,256]{2,1,0:T(8,128)(2,1)S(1)}, bf16[2,256,256]{2,1,0:T(8,128)(2,1)S(1)}) custom-call(s32[2,8]{1,0:T(2,128)S(1)} %copy-done.1, s32[2]{0:T(128)S(1)} %pad_add_fusion.place_ref, bf16[8,640,256]{2,1,0:T(8,128)(2,1)S(1)} %bitcast.5, ...), custom_call_target="tpu_custom_call" | custom-call | flops 1342177280 | bytes 6291456 | tf_op jit(solution)/shard_map/cross/pallas_call | solution.py:183
  80.4 1.0 collective-permute-start.6
  81.4 0.1 collective-permute-done.2.refs_0_
  81.5 4.2 %collective-permute-start.7 = (bf16[2,256,256]{2,1,0:T(8,128)(2,1)S(1)}, bf16[2,256,256]{2,1,0:T(8,128)(2,1)S(1)}, u32[]{:S(2)}, u32[]{:S(2)}) collective-permute-start(bf16[2,256,256]{2,1,0:T(8,128)(2,1)S(1)} %get-tuple-element.44), channel_id=1, source_target_pairs={{0,0},{1,64},{16,16},{17,80},{32,32},{33,96},{48,48},{49,112},{64,... | collective-permute-start | bytes 786440 | tf_op jit(solution)/shard_map/ppermute | solution.py:257
  85.7 2.9 %collective-permute-start.8 = (bf16[2,256,256]{2,1,0:T(8,128)(2,1)S(1)}, bf16[2,256,256]{2,1,0:T(8,128)(2,1)S(1)}, u32[]{:S(2)}, u32[]{:S(2)}) collective-permute-start(bf16[2,256,256]{2,1,0:T(8,128)(2,1)S(1)} %get-tuple-element.45), channel_id=1, source_target_pairs={{0,112},{1,48},{16,96},{17,32},{32,80},{33,16},{48,64},{49,0},{64,... | collective-permute-start | bytes 786440 | tf_op jit(solution)/shard_map/ppermute | solution.py:257
  88.6 2.8 %collective-permute-start.9 = (bf16[2,256,256]{2,1,0:T(8,128)(2,1)S(1)}, bf16[2,256,256]{2,1,0:T(8,128)(2,1)S(1)}, u32[]{:S(2)}, u32[]{:S(2)}) collective-permute-start(bf16[2,256,256]{2,1,0:T(8,128)(2,1)S(1)} %get-tuple-element.46), channel_id=1, source_target_pairs={{0,64},{1,0},{16,80},{17,16},{32,96},{33,32},{48,112},{49,48},{64,... | collective-permute-start | bytes 786440 | tf_op jit(solution)/shard_map/ppermute | solution.py:257
  91.4 1.2 %collective-permute-done.6.refs_4_ = bf16[2,256,256]{2,1,0:T(8,128)(2,1)S(1)} collective-permute-done((bf16[2,256,256]{2,1,0:T(8,128)(2,1)S(1)}, bf16[2,256,256]{2,1,0:T(8,128)(2,1)S(1)}, u32[]{:S(2)}, u32[]{:S(2)}) %collective-permute-start.6) | collective-permute-done | bytes 262176 | tf_op jit(solution)/shard_map/ppermute | solution.py:257
  92.6 2.7 %collective-permute-done.7.refs_5_ = bf16[2,256,256]{2,1,0:T(8,128)(2,1)S(1)} collective-permute-done((bf16[2,256,256]{2,1,0:T(8,128)(2,1)S(1)}, bf16[2,256,256]{2,1,0:T(8,128)(2,1)S(1)}, u32[]{:S(2)}, u32[]{:S(2)}) %collective-permute-start.7) | collective-permute-done | bytes 262176 | tf_op jit(solution)/shard_map/ppermute | solution.py:257
  95.3 4.0 %collective-permute-done.8.refs_6_ = bf16[2,256,256]{2,1,0:T(8,128)(2,1)S(1)} collective-permute-done((bf16[2,256,256]{2,1,0:T(8,128)(2,1)S(1)}, bf16[2,256,256]{2,1,0:T(8,128)(2,1)S(1)}, u32[]{:S(2)}, u32[]{:S(2)}) %collective-permute-start.8) | collective-permute-done | bytes 262176 | tf_op jit(solution)/shard_map/ppermute | solution.py:257
  99.3 0.5 collective-permute-done.9.refs_7_
  99.8 2.6 %join.1 = f32[4,2,2,256,256]{4,3,2,1,0:T(8,128)} custom-call(s32[2]{0:T(128)S(1)} %pad_add_fusion.place_ref, bf16[2,256,256]{2,1,0:T(8,128)(2,1)S(1)} %collective-permute-done.2.refs_0_, bf16[2,256,256]{2,1,0:T(8,128)(2,1)S(1)} %collective-permute-done.3.refs_1_, bf16[2,256,256]{2,1,0:T(8,128)(2,1)S(1)} %collective-permute-done.4.refs_2_, ...), custom_call_target="tpu_custom_call" | custom-call | tf_op jit(solution)/shard_map/join/pallas_call | solution.py:214
  (10 shorter events, 0.0 us)
Async XLA Ops:
  0.8 7.3 %collective-permute-start = (bf16[256,128]{1,0:T(8,128)(2,1)S(1)}, bf16[256,128]{1,0:T(8,128)(2,1)S(1)}, u32[]{:S(2)}, u32[]{:S(2)}) collective-permute-start(bf16[256,128]{1,0:T(8,128)(2,1)S(1)} %slice.3), channel_id=1, source_target_pairs={{0,1},{1,2},{2,3},{3,4},{4,5},{5,6},{6,7},{7,8},{8,9},{9,10},{10,1... | collective-permute-start | bytes 196616 | tf_op jit(solution)/shard_map/ppermute | solution.py:235
  5.4 0.9 copy-start
  6.3 0.7 copy-start.2
  15.8 52.0 %copy-start.1 = (s32[2,8]{1,0:T(2,128)S(1)}, s32[2,8]{1,0:T(2,128)}, u32[]{:S(2)}) copy-start(s32[2,8]{1,0:T(2,128)} %plan_ref.3) | copy-start | bytes 196
  60.7 7.1 %collective-permute-start.1 = (bf16[8,640,256]{2,1,0:T(8,128)(2,1)S(1)}, bf16[8,640,256]{2,1,0:T(8,128)(2,1)}, u32[]{:S(2)}, u32[]{:S(2)}) collective-permute-start(bf16[8,640,256]{2,1,0:T(8,128)(2,1)S(1)} %bitcast.3), channel_id=1, source_target_pairs={{0,1},{1,0},{2,3},{3,2},{4,5},{5,4},{6,7},{7,6},{8,9},{9,8},{10,11... | collective-permute-start | bytes 7864328 | tf_op jit(solution)/shard_map/ppermute | solution.py:243
  71.1 10.4 %collective-permute-start.2 = (bf16[2,256,256]{2,1,0:T(8,128)(2,1)S(1)}, bf16[2,256,256]{2,1,0:T(8,128)(2,1)S(1)}, u32[]{:S(2)}, u32[]{:S(2)}) collective-permute-start(bf16[2,256,256]{2,1,0:T(8,128)(2,1)S(1)} %get-tuple-element.33), channel_id=1, source_target_pairs={{0,16},{1,80},{16,0},{17,64},{32,48},{33,112},{48,32},{49,96},{64,... | collective-permute-start | bytes 786440 | tf_op jit(solution)/shard_map/ppermute | solution.py:257
  73.1 12.6 %collective-permute-start.3 = (bf16[2,256,256]{2,1,0:T(8,128)(2,1)S(1)}, bf16[2,256,256]{2,1,0:T(8,128)(2,1)S(1)}, u32[]{:S(2)}, u32[]{:S(2)}) collective-permute-start(bf16[2,256,256]{2,1,0:T(8,128)(2,1)S(1)} %get-tuple-element.34), channel_id=1, source_target_pairs={{0,32},{1,96},{16,48},{17,112},{32,0},{33,64},{48,16},{49,80},{64,... | collective-permute-start | bytes 786440 | tf_op jit(solution)/shard_map/ppermute | solution.py:257
  73.1 15.5 %collective-permute-start.4 = (bf16[2,256,256]{2,1,0:T(8,128)(2,1)S(1)}, bf16[2,256,256]{2,1,0:T(8,128)(2,1)S(1)}, u32[]{:S(2)}, u32[]{:S(2)}) collective-permute-start(bf16[2,256,256]{2,1,0:T(8,128)(2,1)S(1)} %get-tuple-element.35), channel_id=1, source_target_pairs={{0,48},{1,112},{16,32},{17,96},{32,16},{33,80},{48,0},{49,64},{64,... | collective-permute-start | bytes 786440 | tf_op jit(solution)/shard_map/ppermute | solution.py:257
  77.1 14.3 %collective-permute-start.5 = (bf16[2,256,256]{2,1,0:T(8,128)(2,1)S(1)}, bf16[2,256,256]{2,1,0:T(8,128)(2,1)S(1)}, u32[]{:S(2)}, u32[]{:S(2)}) collective-permute-start(bf16[2,256,256]{2,1,0:T(8,128)(2,1)S(1)} %get-tuple-element.36), channel_id=1, source_target_pairs={{0,96},{1,32},{16,112},{17,48},{32,64},{33,0},{48,80},{49,16},{64,... | collective-permute-start | bytes 786440 | tf_op jit(solution)/shard_map/ppermute | solution.py:257
  80.4 12.2 %collective-permute-start.6 = (bf16[2,256,256]{2,1,0:T(8,128)(2,1)S(1)}, bf16[2,256,256]{2,1,0:T(8,128)(2,1)S(1)}, u32[]{:S(2)}, u32[]{:S(2)}) collective-permute-start(bf16[2,256,256]{2,1,0:T(8,128)(2,1)S(1)} %get-tuple-element.43), channel_id=1, source_target_pairs={{0,80},{1,16},{16,64},{17,0},{32,112},{33,48},{48,96},{49,32},{64,... | collective-permute-start | bytes 786440 | tf_op jit(solution)/shard_map/ppermute | solution.py:257
  81.5 13.8 %collective-permute-start.7 = (bf16[2,256,256]{2,1,0:T(8,128)(2,1)S(1)}, bf16[2,256,256]{2,1,0:T(8,128)(2,1)S(1)}, u32[]{:S(2)}, u32[]{:S(2)}) collective-permute-start(bf16[2,256,256]{2,1,0:T(8,128)(2,1)S(1)} %get-tuple-element.44), channel_id=1, source_target_pairs={{0,0},{1,64},{16,16},{17,80},{32,32},{33,96},{48,48},{49,112},{64,... | collective-permute-start | bytes 786440 | tf_op jit(solution)/shard_map/ppermute | solution.py:257
  85.7 13.6 %collective-permute-start.8 = (bf16[2,256,256]{2,1,0:T(8,128)(2,1)S(1)}, bf16[2,256,256]{2,1,0:T(8,128)(2,1)S(1)}, u32[]{:S(2)}, u32[]{:S(2)}) collective-permute-start(bf16[2,256,256]{2,1,0:T(8,128)(2,1)S(1)} %get-tuple-element.45), channel_id=1, source_target_pairs={{0,112},{1,48},{16,96},{17,32},{32,80},{33,16},{48,64},{49,0},{64,... | collective-permute-start | bytes 786440 | tf_op jit(solution)/shard_map/ppermute | solution.py:257
  88.6 11.2 %collective-permute-start.9 = (bf16[2,256,256]{2,1,0:T(8,128)(2,1)S(1)}, bf16[2,256,256]{2,1,0:T(8,128)(2,1)S(1)}, u32[]{:S(2)}, u32[]{:S(2)}) collective-permute-start(bf16[2,256,256]{2,1,0:T(8,128)(2,1)S(1)} %get-tuple-element.46), channel_id=1, source_target_pairs={{0,64},{1,0},{16,80},{17,16},{32,96},{33,32},{48,112},{49,48},{64,... | collective-permute-start | bytes 786440 | tf_op jit(solution)/shard_map/ppermute | solution.py:257

commit v3 on v2

--- a/solution.py
+++ b/solution.py
@@ -15,11 +15,14 @@
 TAPS = 64
 ROUNDS = 2
 STEP_WINDOWS = 8
+FIRST_PARTS = 4
 PIECES = 3
 TILE = 16
-VMEM = 50 * 1024 * 1024
+VMEM = 32 * 1024 * 1024
 SMALL_VMEM = 8 * 1024 * 1024
-CALLS = ((2, 4, 6, 5), (3, 0, 7, 1))
+FIRST = 2
+CALLS = ((6, 4, 3), (7, 5, 0, 1))
+JOINED_EARLY = 5
 
 
 def dft_rows(chips, blocks):
@@ -39,13 +42,23 @@
     return pieces
 
 
-def table_kernel(taps_ref, dft_ref, main_ref, before_ref, order_ref):
+def table_kernel(taps_at, dft_at, main_ref, before_ref, order_ref, taps_ref, dft_ref, sems):
+    taps_copy = pltpu.make_async_copy(taps_at, taps_ref, sems.at[0])
+    dft_copy = pltpu.make_async_copy(dft_at, dft_ref, sems.at[1])
+    taps_copy.start()
+    dft_copy.start()
+    row = lax.broadcasted_iota(jnp.int32, order_ref.shape, 0)
+    column = lax.broadcasted_iota(jnp.int32, order_ref.shape, 1)
+    source = (row & 7) * 32 + ((row >> 3) & 1) * 16 + (row >> 4)
+    order_ref[...] = jnp.where(column == source, 1.0, 0.0).astype(jnp.bfloat16)
+    taps_copy.wait()
     lane = lax.broadcasted_iota(jnp.int32, (1, 2 * WL), 1)
     reversed_taps = jnp.zeros((1, 2 * WL), jnp.float32)
     for tap in range(TAPS):
         reversed_taps = jnp.where(lane == TAPS - 1 - tap, taps_ref[tap], reversed_taps)
     spread = jnp.broadcast_to(reversed_taps, (WL, 2 * WL))
     toeplitz = pltpu.roll(spread, WL - TAPS + 1, 1, stride=1, stride_axis=0)
+    dft_copy.wait()
     combined = jnp.dot(
         dft_ref[...], toeplitz, precision=lax.Precision.HIGHEST, preferred_element_type=jnp.float32
     )
@@ -55,10 +68,6 @@
     first = jnp.where(left, pltpu.roll(high, TAPS, 1), middle)
     second = jnp.where(left, pltpu.roll(low, TAPS, 1), 0.0)
     before_ref[...] = jnp.concatenate([first, second], axis=1).astype(jnp.bfloat16)
-    row = lax.broadcasted_iota(jnp.int32, order_ref.shape, 0)
-    column = lax.broadcasted_iota(jnp.int32, order_ref.shape, 1)
-    source = (row & 7) * 32 + ((row >> 3) & 1) * 16 + (row >> 4)
-    order_ref[...] = jnp.where(column == source, 1.0, 0.0).astype(jnp.bfloat16)
 
 
 IN_VMEM = pl.BlockSpec(memory_space=pltpu.VMEM)
@@ -71,11 +80,16 @@
     return pl.pallas_call(
         table_kernel,
         out_shape=[jax.ShapeDtypeStruct((count, WL), jnp.bfloat16) for count in rows],
-        in_specs=[IN_SMEM, IN_VMEM],
+        in_specs=[IN_HBM, IN_HBM],
         out_specs=[IN_VMEM] * 3,
+        scratch_shapes=[
+            pltpu.SMEM(fir_taps.shape, jnp.float32),
+            pltpu.VMEM(dft.shape, jnp.float32),
+            pltpu.SemaphoreType.DMA((2,)),
+        ],
         compiler_params=pltpu.CompilerParams(vmem_limit_bytes=SMALL_VMEM),
         name="table",
-    )(fir_taps, dft)
+    )(*(pltpu.with_memory_space_constraint(given, pltpu.HBM) for given in (fir_taps, dft)))
 
 
 NT = (((1,), (1,)), ((), ()))
@@ -87,28 +101,47 @@
 
 
 def spectra_kernel(
-    tail_ref, main_ref, before_ref, order_ref, records_ref, out_ref, samples_ref, carry_ref, held_ref, sems
+    tail_ref,
+    main_ref,
+    before_ref,
+    order_ref,
+    records_ref,
+    out_ref,
+    samples_ref,
+    carry_ref,
+    held_ref,
+    white_ref,
+    in_sems,
+    out_sems,
 ):
     groups = samples_ref.shape[0]
     width = STEP_WINDOWS * WL
+    first = width // FIRST_PARTS
     count = 2 * F
+    before = before_ref[...]
+
+    def fetch_first(part):
+        lanes = pl.ds(part * first, first)
+        return pltpu.make_async_copy(
+            records_ref.at[:, lanes], samples_ref.at[0, :, lanes], in_sems.at[groups + part]
+        )
 
     def fetch(group):
         source = records_ref.at[:, pl.ds(pl.multiple_of(group * width, width), width)]
-        return pltpu.make_async_copy(source, samples_ref.at[group], sems.at[group])
-
-    for group in range(groups):
-        fetch(group).start()
-    before = before_ref[...]
-    carry_ref[...] = lax.dot_general(
-        before, last_samples(tail_ref[...]), NT, preferred_element_type=jnp.float32
-    )
-
-    @pl.loop(0, groups)
-    def _(group):
-        fetch(group).wait()
+        return pltpu.make_async_copy(source, samples_ref.at[group], in_sems.at[group])
+
+    def rows_of(group):
+        return pl.ds(pl.multiple_of(group * TILE, TILE), TILE)
+
+    def send(group):
+        at = rows_of(group)
+        return pltpu.make_async_copy(white_ref.at[:, at, :], out_ref.at[:, at, :], out_sems.at[group])
+
+    def make(group):
         carry = carry_ref[...]
         for inner in range(STEP_WINDOWS):
+            if isinstance(group, int) and inner * WL % first == 0:
+                fetch_first(inner * WL // first).wait()
             samples = samples_ref[group, :, inner * WL : (inner + 1) * WL]
             rows = lax.dot_general(main_ref[...], samples, NT, preferred_element_type=jnp.float32)
             stacked = rows[2 * count :] + rows[count : 2 * count] + carry + rows[:count]
@@ -118,6 +151,8 @@
             power = jnp.sum(stacked * stacked, axis=0, keepdims=True) * (1.0 / count) + 1e-06
             held_ref[inner] = (stacked * (1.0 / jnp.sqrt(power))).astype(jnp.bfloat16)
         carry_ref[...] = carry
+
+    def place(group):
         for part in range(F // TILE):
             rows = []
             for inner in range(STEP_WINDOWS):
@@ -126,28 +161,51 @@
             placed = jnp.dot(
                 order_ref[...], jnp.concatenate(rows, axis=0), preferred_element_type=jnp.float32
             ).astype(jnp.bfloat16)
-            at = pl.ds(pl.multiple_of(group * TILE, TILE), TILE)
             for n in range(TILE):
-                out_ref[part * TILE + n, at, :] = placed[n * TILE : (n + 1) * TILE]
+                white_ref[part * TILE + n, rows_of(group), :] = placed[n * TILE : (n + 1) * TILE]
+
+    for part in range(FIRST_PARTS):
+        fetch_first(part).start()
+    for group in range(1, groups):
+        fetch(group).start()
+    carry_ref[...] = lax.dot_general(
+        before, last_samples(tail_ref[...]), NT, preferred_element_type=jnp.float32
+    )
+    make(0)
+
+    @pl.loop(1, groups)
+    def _(group):
+        fetch(group).wait()
+        place(group - 1)
+        make(group)
+        send(group - 1).start()
+
+    place(groups - 1)
+    send(groups - 1).start()
+    for group in range(groups):
+        send(group).wait()
 
 
 def spectra(tail, tables, records):
     channels, samples = records.shape
     groups = samples // WL // STEP_WINDOWS
+    result = (F, groups * TILE, channels)
     return pl.pallas_call(
         spectra_kernel,
-        out_shape=jax.ShapeDtypeStruct((F, groups * TILE, channels), jnp.bfloat16),
+        out_shape=pltpu.HBM(result, jnp.bfloat16),
         in_specs=[IN_VMEM] * 4 + [IN_HBM],
-        out_specs=IN_VMEM,
+        out_specs=IN_HBM,
         scratch_shapes=[
             pltpu.VMEM((groups, channels, STEP_WINDOWS * WL), jnp.bfloat16),
             pltpu.VMEM((2 * F, channels), jnp.float32),
             pltpu.VMEM((STEP_WINDOWS, 2 * F, channels), jnp.bfloat16),
+            pltpu.VMEM(result, jnp.bfloat16),
+            pltpu.SemaphoreType.DMA((groups + FIRST_PARTS,)),
             pltpu.SemaphoreType.DMA((groups,)),
         ],
         compiler_params=pltpu.CompilerParams(vmem_limit_bytes=VMEM),
         name="spectra",
-    )(tail, *tables, records)
+    )(tail, *tables, pltpu.with_memory_space_constraint(records, pltpu.HBM))
 
 
 def rotated(rows):
@@ -166,13 +224,15 @@
     return place ^ (step // 2) ^ (half * ((step % 2) ^ core))
 
 
-def cross_kernel(scale, steps, plan_ref, place_ref, here_ref, other_ref, *out_refs):
+def cross_kernel(scale, steps, plan_ref, place_ref, here_ref, other_ref, *refs):
     half_blocks = here_ref.shape[0] // 2
+    picked = other_ref.shape[0] == 2
+    out_refs = refs[-len(steps) :]
     for step, out_ref in zip(steps, out_refs):
         own_at = target(step, half_blocks, place_ref[0], place_ref[1])
         mate_at = plan_ref[place_ref[1], own_at]
-        own = jnp.concatenate([here_ref[own_at], other_ref[own_at]], axis=0)
-        mate = jnp.concatenate([here_ref[mate_at], other_ref[mate_at]], axis=0)
+        own = jnp.concatenate([here_ref[own_at], other_ref[0 if picked else own_at]], axis=0)
+        mate = jnp.concatenate([here_ref[mate_at], other_ref[1 if picked else mate_at]], axis=0)
         for half, rows in enumerate((own, rotated(own))):
             product = lax.dot_general(mate, rows, TN, preferred_element_type=jnp.float32) * scale
             out_ref[half] = product.astype(jnp.bfloat16)
@@ -196,7 +256,7 @@
 
 
 def join_kernel(steps, bins, place_ref, *refs):
-    parts, (out_ref, wide_ref, sems) = refs[:-3], refs[-3:]
+    parts, (out_ref, wide_ref, sems) = refs[: len(steps)], refs[-3:]
     copies = []
     for n, step in enumerate(steps):
         own_bin = (place_ref[0] % bins) ^ (step // 2)
@@ -209,20 +269,24 @@
         copy.wait()
 
 
-def join(steps, place, parts, bins):
+def join(steps, place, parts, bins, earlier=()):
     halves, rows, channels = parts[0].shape
     return pl.pallas_call(
         functools.partial(join_kernel, steps, bins),
-        in_specs=[IN_SMEM] + [IN_VMEM] * len(steps),
-        out_specs=pl.BlockSpec(memory_space=pl.ANY),
+        in_specs=[IN_SMEM] + [IN_VMEM] * len(steps) + [IN_HBM] * len(earlier),
+        out_specs=IN_HBM,
         out_shape=jax.ShapeDtypeStruct((bins, ROUNDS, halves, rows, channels), jnp.float32),
         scratch_shapes=[
             pltpu.VMEM((len(steps), halves, rows, channels), jnp.float32),
             pltpu.SemaphoreType.DMA((len(steps),)),
         ],
+        input_output_aliases={1 + len(steps): 0} if earlier else {},
         compiler_params=pltpu.CompilerParams(vmem_limit_bytes=SMALL_VMEM),
+        cost_estimate=pl.CostEstimate(
+            flops=0, bytes_accessed=len(steps) * 6 * halves * rows * channels, transcendentals=0
+        ),
         name="join",
-    )(place, *parts)
+    )(place, *parts, *earlier)
 
 
 def on_device(dft, records, fir_taps, plan):
@@ -240,14 +304,21 @@
     white = spectra(tail, make_tables(fir_taps, dft), records)
     here = lax.all_to_all(white, ("chan", "chip"), 0, 0, tiled=True)
     here = here.reshape(blocks, chips * white.shape[1], channels)
-    other = lax.ppermute(here, "core", swap)
     half = blocks // 2
     place = jnp.stack([lax.axis_index("chan").astype(jnp.int32), core])
-    steps = [step for call in CALLS for step in call]
+    away_at = target(FIRST, half, place[0], 1 - core)
+    away = [here[away_at], here[plan[1 - core, away_at]]]
+    first_other = lax.ppermute(jnp.stack(away), "core", swap)
+    here, first_other = lax.optimization_barrier((here, first_other))
+    other = lax.ppermute(here, "core", swap)
     parts = []
-    for call in CALLS:
-        products = cross(call, plan, place, here, other, scale)
-        here, other, *products = lax.optimization_barrier((here, other, *products))
+    last = ()
+    for call in ((FIRST,), *CALLS):
+        products = cross(call, plan, place, here, first_other if call == (FIRST,) else other, scale)
+        if call == (FIRST,):
+            here, *products = lax.optimization_barrier((here, *products))
+        else:
+            here, other, *products = lax.optimization_barrier((here, other, *products))
         for step, product in zip(call, products):
             route = [
                 (j * cores + h, target(step, half, j, h) * cores + j // half)
@@ -255,7 +326,10 @@
                 for h in range(cores)
             ]
             parts.append(lax.ppermute(product, ("chan", "core"), route))
-    return join(steps, place, parts, half)
+    steps = [FIRST] + [step for call in CALLS for step in call]
+    if JOINED_EARLY:
+        last = [join(steps[:JOINED_EARLY], place, parts[:JOINED_EARLY], half)]
+    return join(steps[JOINED_EARLY:], place, parts[JOINED_EARLY:], half, last)
 
 
 def solution(mesh):

time: 103 us -> 99.1 us (0.962)
  blocking collectives: 44.9 us -> 0 us
  waiting for transfers between devices: 13.1 us -> 39.2 us
  starting transfers between devices: 23.8 us -> 37.1 us
  between operations: 0.11 us -> 2.22 us
    all_to_all x1 -> x0, blocking collectives: 44.9 us -> none  [on_device(): here = lax.all_to_all(white, ('chan', 'chip'), 0, 0, tiled=True)]
    all_to_all x0 -> x1, waiting for transfers between devices: none -> 30.1 us  [on_device(): here = lax.all_to_all(white, ('chan', 'chip'), 0, 0, tiled=True)]
    all_to_all x0 -> x1, starting transfers between devices: none -> 10.8 us  [on_device(): here = lax.all_to_all(white, ('chan', 'chip'), 0, 0, tiled=True)]
    ppermute x1, waiting for transfers between devices: 4.59 us -> 0.32 us  [on_device(): other = lax.ppermute(here, 'core', swap)]
    ppermute x0 -> x1, starting transfers between devices: none -> 3.96 us  [on_device(): first_other = lax.ppermute(jnp.stack(away), 'core', swap)]
    ppermute x1, starting transfers between devices: 2.42 us -> 0.37 us  [on_device(): other = lax.ppermute(here, 'core', swap)]
    ppermute x0 -> x1, waiting for transfers between devices: none -> 1.72 us  [on_device(): first_other = lax.ppermute(jnp.stack(away), 'core', swap)]
    pallas_call x2 -> x3, Pallas kernels: 6.6 us -> 4.96 us  [cross(): pl.pallas_call(functools.partial(cross_kernel, scale, steps), in_specs=[I...]
  transfers between devices with their start and end apart: 10 -> 12, of which waited for: 6 -> 7; matrix products, arithmetic and copies ran while one was open for 0% -> 1% of each run, Pallas kernels for 4% -> 9%
where the time goes in v3:
time: 99.1 us; the launch traced here: 98.7 us
  waiting for transfers between devices  39.2 us (40%)
  starting transfers between devices  37.1 us (37%)
  Pallas kernels  18.5 us (19%)
  between operations  2.22 us (2%)
  local copies, waits for them, and re-layouts  1.56 us (2%)
    all_to_all x1, waiting for transfers between devices, on_device(): here = lax.all_to_all(white, ('chan', 'chip'), 0, 0, tiled=True)  30.1 us
    ppermute x8, starting transfers between devices, on_device(): parts.append(lax.ppermute(product, ('chan', 'core'), route))  17.3 us
    all_to_all x1, starting transfers between devices, on_device(): here = lax.all_to_all(white, ('chan', 'chip'), 0, 0, tiled=True)  10.8 us
    pallas_call x1, Pallas kernels, spectra(): pl.pallas_call(spectra_kernel, out_shape=pltpu.HBM(result, jnp.bfloat16),...  8.25 us
    ppermute x8, waiting for transfers between devices, on_device(): parts.append(lax.ppermute(product, ('chan', 'core'), route))  7.06 us
    pallas_call x3, Pallas kernels, cross(): pl.pallas_call(functools.partial(cross_kernel, scale, steps), in_specs=[I...  4.96 us
    ppermute x1, starting transfers between devices, on_device(): lax.ppermute(records[:, samples_here - WL // 2:], ('chip', 'core'), [(i,...  4.58 us
    ppermute x1, starting transfers between devices, on_device(): first_other = lax.ppermute(jnp.stack(away), 'core', swap)  3.96 us
  transfers between devices with their start and end apart: 12, of which 7 were waited for; matrix products, arithmetic and copies ran while one was open for 1% of the time, Pallas kernels for 9%

profile of v3, /device:TPU:1, one launch (start us, length us, event | category | flops | bytes accessed | tf_op | source)
XLA Modules:
  0.0 98.7 jit_solution(15043487647635752397)
XLA Ops:
  0.0 0.8 slice.3
  0.8 4.6 %collective-permute-start = (bf16[256,128]{1,0:T(8,128)(2,1)S(1)}, bf16[256,128]{1,0:T(8,128)(2,1)S(1)}, u32[]{:S(2)}, u32[]{:S(2)}) collective-permute-start(bf16[256,128]{1,0:T(8,128)(2,1)S(1)} %slice.3), channel_id=1, source_target_pairs={{0,1},{1,2},{2,3},{3,4},{4,5},{5,6},{6,7},{7,8},{8,9},{9,10},{10,1... | collective-permute-start | bytes 196616 | tf_op jit(solution)/shard_map/ppermute | solution.py:299
  5.4 1.4 %table.1 = (bf16[384,256]{1,0:T(8,128)(2,1)S(1)}, bf16[128,256]{1,0:T(8,128)(2,1)S(1)}, bf16[256,256]{1,0:T(8,128)(2,1)S(1)}) custom-call(f32[64]{0:T(128)} %taps_at.1, f32[128,256]{1,0:T(8,128)} %constant.23.clone.dft_at), custom_call_target="tpu_custom_call" | custom-call | tf_op jit(solution)/shard_map/table/pallas_call | solution.py:80
  6.9 8.3 %spectra.1 = bf16[64,80,256]{2,1,0:T(8,128)(2,1)} custom-call(bf16[256,128]{1,0:T(8,128)(2,1)S(1)} %collective-permute-done.tail_ref, bf16[384,256]{1,0:T(8,128)(2,1)S(1)} %get-tuple-element.28.main_ref, bf16[128,256]{1,0:T(8,128)(2,1)S(1)} %get-tuple-element.29.before_ref, bf16[256,256]{1,0:T(8,128)(2,1)S(1)} %get-tuple-element.30.order_ref, ...), custom_call_target="tpu_custom_call" | custom-call | tf_op jit(solution)/shard_map/spectra/pallas_call | solution.py:193
  15.1 10.8 %all-to-all-start = ((bf16[64,80,256]{2,1,0:T(8,128)(2,1)}), bf16[64,80,256]{2,1,0:T(8,128)(2,1)S(1)}, u32[]{:S(2)}, u32[]{:S(2)}) async-start(bf16[64,80,256]{2,1,0:T(8,128)(2,1)} %spectra.1), calls=%async_computation | async-start | bytes 5242880 | tf_op jit(solution)/shard_map/all_to_all | solution.py:305
  26.0 0.7 dynamic_slice.10
  28.8 30.1 %all-to-all-done = bf16[64,80,256]{2,1,0:T(8,128)(2,1)S(1)} async-done(((bf16[64,80,256]{2,1,0:T(8,128)(2,1)}), bf16[64,80,256]{2,1,0:T(8,128)(2,1)S(1)}, u32[]{:S(2)}, u32[]{:S(2)}) %all-to-all-start) | async-done | bytes 2621472 | tf_op jit(solution)/shard_map/all_to_all | solution.py:305
  59.0 4.0 %collective-permute-start.1 = (bf16[2,640,256]{2,1,0:T(8,128)(2,1)S(1)}, bf16[2,640,256]{2,1,0:T(8,128)(2,1)S(1)}, u32[]{:S(2)}, u32[]{:S(2)}) collective-permute-start(bf16[2,640,256]{2,1,0:T(8,128)(2,1)S(1)} %pad_maximum_fusion), channel_id=1, source_target_pairs={{0,1},{1,0},{2,3},{3,2},{4,5},{5,4},{6,7},{7,6},{8,9},{9,8},{10,11... | collective-permute-start | bytes 1966088 | tf_op jit(solution)/shard_map/ppermute | solution.py:311
  63.0 1.7 %collective-permute-done.1.other_ref = bf16[2,640,256]{2,1,0:T(8,128)(2,1)S(1)} collective-permute-done((bf16[2,640,256]{2,1,0:T(8,128)(2,1)S(1)}, bf16[2,640,256]{2,1,0:T(8,128)(2,1)S(1)}, u32[]{:S(2)}, u32[]{:S(2)}) %collective-permute-start.1) | collective-permute-done | bytes 655392 | tf_op jit(solution)/shard_map/ppermute | solution.py:311
  65.2 1.1 %cross.3 = bf16[2,256,256]{2,1,0:T(8,128)(2,1)S(1)} custom-call(s32[2,8]{1,0:T(2,128)S(1)} %copy-done, s32[2]{0:T(128)S(1)} %pad_add_fusion.place_ref, bf16[8,640,256]{2,1,0:T(8,128)(2,1)S(1)} %bitcast.6, bf16[2,640,256]{2,1,0:T(8,128)(2,1)S(1)} %collective-permute-done.1.other_ref), custom_call_target="tpu_custom_call" | custom-call | flops 335544320 | bytes 1572864 | tf_op jit(solution)/shard_map/cross/pallas_call | solution.py:243
  66.3 3.0 %collective-permute-start.6 = (bf16[2,256,256]{2,1,0:T(8,128)(2,1)S(1)}, bf16[2,256,256]{2,1,0:T(8,128)(2,1)S(1)}, u32[]{:S(2)}, u32[]{:S(2)}) collective-permute-start(bf16[2,256,256]{2,1,0:T(8,128)(2,1)S(1)} %cross.3), channel_id=1, source_target_pairs={{0,16},{1,80},{16,0},{17,64},{32,48},{33,112},{48,32},{49,96},{64,... | collective-permute-start | bytes 786440 | tf_op jit(solution)/shard_map/ppermute | solution.py:328
  69.6 1.8 %cross.4 = (bf16[2,256,256]{2,1,0:T(8,128)(2,1)S(1)}, bf16[2,256,256]{2,1,0:T(8,128)(2,1)S(1)}, bf16[2,256,256]{2,1,0:T(8,128)(2,1)S(1)}) custom-call(s32[2,8]{1,0:T(2,128)S(1)} %copy-done, s32[2]{0:T(128)S(1)} %pad_add_fusion.place_ref, bf16[8,640,256]{2,1,0:T(8,128)(2,1)S(1)} %bitcast.7, bf16[8,640,256]{2,1,0:T(8,128)(2,1)S(1)} %collective-permute-done.2.other_ref), custom_call_target="tpu_custom_call" | custom-call | flops 1006632960 | bytes 4718592 | tf_op jit(solution)/shard_map/cross/pallas_call | solution.py:243
  71.4 1.3 %collective-permute-start.7 = (bf16[2,256,256]{2,1,0:T(8,128)(2,1)S(1)}, bf16[2,256,256]{2,1,0:T(8,128)(2,1)S(1)}, u32[]{:S(2)}, u32[]{:S(2)}) collective-permute-start(bf16[2,256,256]{2,1,0:T(8,128)(2,1)S(1)} %get-tuple-element.47), channel_id=1, source_target_pairs={{0,48},{1,112},{16,32},{17,96},{32,16},{33,80},{48,0},{49,64},{64,... | collective-permute-start | bytes 786440 | tf_op jit(solution)/shard_map/ppermute | solution.py:328
  72.7 2.3 %collective-permute-start.8 = (bf16[2,256,256]{2,1,0:T(8,128)(2,1)S(1)}, bf16[2,256,256]{2,1,0:T(8,128)(2,1)S(1)}, u32[]{:S(2)}, u32[]{:S(2)}) collective-permute-start(bf16[2,256,256]{2,1,0:T(8,128)(2,1)S(1)} %get-tuple-element.48), channel_id=1, source_target_pairs={{0,32},{1,96},{16,48},{17,112},{32,0},{33,64},{48,16},{49,80},{64,... | collective-permute-start | bytes 786440 | tf_op jit(solution)/shard_map/ppermute | solution.py:328
  75.0 1.5 %collective-permute-start.9 = (bf16[2,256,256]{2,1,0:T(8,128)(2,1)S(1)}, bf16[2,256,256]{2,1,0:T(8,128)(2,1)S(1)}, u32[]{:S(2)}, u32[]{:S(2)}) collective-permute-start(bf16[2,256,256]{2,1,0:T(8,128)(2,1)S(1)} %get-tuple-element.49), channel_id=1, source_target_pairs={{0,80},{1,16},{16,64},{17,0},{32,112},{33,48},{48,96},{49,32},{64,... | collective-permute-start | bytes 786440 | tf_op jit(solution)/shard_map/ppermute | solution.py:328
  76.4 2.1 %cross.5 = (bf16[2,256,256]{2,1,0:T(8,128)(2,1)S(1)}, bf16[2,256,256]{2,1,0:T(8,128)(2,1)S(1)}, bf16[2,256,256]{2,1,0:T(8,128)(2,1)S(1)}, bf16[2,256,256]{2,1,0:T(8,128)(2,1)S(1)}) custom-call(s32[2,8]{1,0:T(2,128)S(1)} %copy-done, s32[2]{0:T(128)S(1)} %pad_add_fusion.place_ref, bf16[8,640,256]{2,1,0:T(8,128)(2,1)S(1)} %bitcast.8, ...), custom_call_target="tpu_custom_call" | custom-call | flops 1342177280 | bytes 6291456 | tf_op jit(solution)/shard_map/cross/pallas_call | solution.py:243
  78.5 0.9 collective-permute-start.3
  79.5 3.3 %collective-permute-start.10 = (bf16[2,256,256]{2,1,0:T(8,128)(2,1)S(1)}, bf16[2,256,256]{2,1,0:T(8,128)(2,1)S(1)}, u32[]{:S(2)}, u32[]{:S(2)}) collective-permute-start(bf16[2,256,256]{2,1,0:T(8,128)(2,1)S(1)} %get-tuple-element.50), channel_id=1, source_target_pairs={{0,112},{1,48},{16,96},{17,32},{32,80},{33,16},{48,64},{49,0},{64,... | collective-permute-start | bytes 786440 | tf_op jit(solution)/shard_map/ppermute | solution.py:328
  83.2 3.1 %collective-permute-start.4 = (bf16[2,256,256]{2,1,0:T(8,128)(2,1)S(1)}, bf16[2,256,256]{2,1,0:T(8,128)(2,1)S(1)}, u32[]{:S(2)}, u32[]{:S(2)}) collective-permute-start(bf16[2,256,256]{2,1,0:T(8,128)(2,1)S(1)} %get-tuple-element.44), channel_id=1, source_target_pairs={{0,0},{1,64},{16,16},{17,80},{32,32},{33,96},{48,48},{49,112},{64,... | collective-permute-start | bytes 786440 | tf_op jit(solution)/shard_map/ppermute | solution.py:328
  86.3 1.9 %collective-permute-start.5 = (bf16[2,256,256]{2,1,0:T(8,128)(2,1)S(1)}, bf16[2,256,256]{2,1,0:T(8,128)(2,1)S(1)}, u32[]{:S(2)}, u32[]{:S(2)}) collective-permute-start(bf16[2,256,256]{2,1,0:T(8,128)(2,1)S(1)} %get-tuple-element.45), channel_id=1, source_target_pairs={{0,64},{1,0},{16,80},{17,16},{32,96},{33,32},{48,112},{49,48},{64,... | collective-permute-start | bytes 786440 | tf_op jit(solution)/shard_map/ppermute | solution.py:328
  88.4 4.4 %collective-permute-done.10.refs_4_ = bf16[2,256,256]{2,1,0:T(8,128)(2,1)S(1)} collective-permute-done((bf16[2,256,256]{2,1,0:T(8,128)(2,1)S(1)}, bf16[2,256,256]{2,1,0:T(8,128)(2,1)S(1)}, u32[]{:S(2)}, u32[]{:S(2)}) %collective-permute-start.10) | collective-permute-done | bytes 262176 | tf_op jit(solution)/shard_map/ppermute | solution.py:328
  92.8 2.1 %join.2.refs_3_ = f32[4,2,2,256,256]{4,3,2,1,0:T(8,128)} custom-call(s32[2]{0:T(128)S(1)} %pad_add_fusion.place_ref, bf16[2,256,256]{2,1,0:T(8,128)(2,1)S(1)} %collective-permute-done.6.refs_0_, bf16[2,256,256]{2,1,0:T(8,128)(2,1)S(1)} %collective-permute-done.7.refs_1_, bf16[2,256,256]{2,1,0:T(8,128)(2,1)S(1)} %collective-permute-done.8.refs_2_, ...), custom_call_target="tpu_custom_call" | custom-call | bytes 3932160 | tf_op jit(solution)/shard_map/join/pallas_call | solution.py:274
  94.9 2.0 %collective-permute-done.3.refs_0_ = bf16[2,256,256]{2,1,0:T(8,128)(2,1)S(1)} collective-permute-done((bf16[2,256,256]{2,1,0:T(8,128)(2,1)S(1)}, bf16[2,256,256]{2,1,0:T(8,128)(2,1)S(1)}, u32[]{:S(2)}, u32[]{:S(2)}) %collective-permute-start.3) | collective-permute-done | bytes 262176 | tf_op jit(solution)/shard_map/ppermute | solution.py:328
  97.0 1.7 %join.3 = f32[4,2,2,256,256]{4,3,2,1,0:T(8,128)} custom-call(s32[2]{0:T(128)S(1)} %pad_add_fusion.place_ref, bf16[2,256,256]{2,1,0:T(8,128)(2,1)S(1)} %collective-permute-done.3.refs_0_, bf16[2,256,256]{2,1,0:T(8,128)(2,1)S(1)} %collective-permute-done.4.refs_1_, ...), custom_call_target="tpu_custom_call", output_to_operand_aliasing={{}: (4, {})} | custom-call | bytes 2359296 | tf_op jit(solution)/shard_map/join/pallas_call | solution.py:274
  (14 shorter events, 1.5 us)
Async XLA Ops:
  0.8 6.0 %collective-permute-start = (bf16[256,128]{1,0:T(8,128)(2,1)S(1)}, bf16[256,128]{1,0:T(8,128)(2,1)S(1)}, u32[]{:S(2)}, u32[]{:S(2)}) collective-permute-start(bf16[256,128]{1,0:T(8,128)(2,1)S(1)} %slice.3), channel_id=1, source_target_pairs={{0,1},{1,2},{2,3},{3,4},{4,5},{5,6},{6,7},{7,8},{8,9},{9,10},{10,1... | collective-permute-start | bytes 196616 | tf_op jit(solution)/shard_map/ppermute | solution.py:299
  15.1 10.9 %copy-start = (s32[2,8]{1,0:T(2,128)S(1)}, s32[2,8]{1,0:T(2,128)}, u32[]{:S(2)}) copy-start(s32[2,8]{1,0:T(2,128)} %plan_ref.5) | copy-start | bytes 196
  15.1 43.8 %all-to-all-start = ((bf16[64,80,256]{2,1,0:T(8,128)(2,1)}), bf16[64,80,256]{2,1,0:T(8,128)(2,1)S(1)}, u32[]{:S(2)}, u32[]{:S(2)}) async-start(bf16[64,80,256]{2,1,0:T(8,128)(2,1)} %spectra.1), calls=%async_computation | async-start | bytes 5242880 | tf_op jit(solution)/shard_map/all_to_all | solution.py:305
  59.0 5.7 %collective-permute-start.1 = (bf16[2,640,256]{2,1,0:T(8,128)(2,1)S(1)}, bf16[2,640,256]{2,1,0:T(8,128)(2,1)S(1)}, u32[]{:S(2)}, u32[]{:S(2)}) collective-permute-start(bf16[2,640,256]{2,1,0:T(8,128)(2,1)S(1)} %pad_maximum_fusion), channel_id=1, source_target_pairs={{0,1},{1,0},{2,3},{3,2},{4,5},{5,4},{6,7},{7,6},{8,9},{9,8},{10,11... | collective-permute-start | bytes 1966088 | tf_op jit(solution)/shard_map/ppermute | solution.py:311
  64.7 4.9 %collective-permute-start.2 = (bf16[8,640,256]{2,1,0:T(8,128)(2,1)S(1)}, bf16[8,640,256]{2,1,0:T(8,128)(2,1)S(1)}, u32[]{:S(2)}, u32[]{:S(2)}) collective-permute-start(bf16[8,640,256]{2,1,0:T(8,128)(2,1)S(1)} %bitcast.5), channel_id=1, source_target_pairs={{0,1},{1,0},{2,3},{3,2},{4,5},{5,4},{6,7},{7,6},{8,9},{9,8},{10,11... | collective-permute-start | bytes 7864328 | tf_op jit(solution)/shard_map/ppermute | solution.py:313
  66.3 13.2 %collective-permute-start.6 = (bf16[2,256,256]{2,1,0:T(8,128)(2,1)S(1)}, bf16[2,256,256]{2,1,0:T(8,128)(2,1)S(1)}, u32[]{:S(2)}, u32[]{:S(2)}) collective-permute-start(bf16[2,256,256]{2,1,0:T(8,128)(2,1)S(1)} %cross.3), channel_id=1, source_target_pairs={{0,16},{1,80},{16,0},{17,64},{32,48},{33,112},{48,32},{49,96},{64,... | collective-permute-start | bytes 786440 | tf_op jit(solution)/shard_map/ppermute | solution.py:328
  71.4 11.8 %collective-permute-start.7 = (bf16[2,256,256]{2,1,0:T(8,128)(2,1)S(1)}, bf16[2,256,256]{2,1,0:T(8,128)(2,1)S(1)}, u32[]{:S(2)}, u32[]{:S(2)}) collective-permute-start(bf16[2,256,256]{2,1,0:T(8,128)(2,1)S(1)} %get-tuple-element.47), channel_id=1, source_target_pairs={{0,48},{1,112},{16,32},{17,96},{32,16},{33,80},{48,0},{49,64},{64,... | collective-permute-start | bytes 786440 | tf_op jit(solution)/shard_map/ppermute | solution.py:328
  72.7 13.6 %collective-permute-start.8 = (bf16[2,256,256]{2,1,0:T(8,128)(2,1)S(1)}, bf16[2,256,256]{2,1,0:T(8,128)(2,1)S(1)}, u32[]{:S(2)}, u32[]{:S(2)}) collective-permute-start(bf16[2,256,256]{2,1,0:T(8,128)(2,1)S(1)} %get-tuple-element.48), channel_id=1, source_target_pairs={{0,32},{1,96},{16,48},{17,112},{32,0},{33,64},{48,16},{49,80},{64,... | collective-permute-start | bytes 786440 | tf_op jit(solution)/shard_map/ppermute | solution.py:328
  75.0 13.4 %collective-permute-start.9 = (bf16[2,256,256]{2,1,0:T(8,128)(2,1)S(1)}, bf16[2,256,256]{2,1,0:T(8,128)(2,1)S(1)}, u32[]{:S(2)}, u32[]{:S(2)}) collective-permute-start(bf16[2,256,256]{2,1,0:T(8,128)(2,1)S(1)} %get-tuple-element.49), channel_id=1, source_target_pairs={{0,80},{1,16},{16,64},{17,0},{32,112},{33,48},{48,96},{49,32},{64,... | collective-permute-start | bytes 786440 | tf_op jit(solution)/shard_map/ppermute | solution.py:328
  78.5 18.4 %collective-permute-start.3 = (bf16[2,256,256]{2,1,0:T(8,128)(2,1)S(1)}, bf16[2,256,256]{2,1,0:T(8,128)(2,1)S(1)}, u32[]{:S(2)}, u32[]{:S(2)}) collective-permute-start(bf16[2,256,256]{2,1,0:T(8,128)(2,1)S(1)} %get-tuple-element.43), channel_id=1, source_target_pairs={{0,96},{1,32},{16,112},{17,48},{32,64},{33,0},{48,80},{49,16},{64,... | collective-permute-start | bytes 786440 | tf_op jit(solution)/shard_map/ppermute | solution.py:328
  79.5 13.3 %collective-permute-start.10 = (bf16[2,256,256]{2,1,0:T(8,128)(2,1)S(1)}, bf16[2,256,256]{2,1,0:T(8,128)(2,1)S(1)}, u32[]{:S(2)}, u32[]{:S(2)}) collective-permute-start(bf16[2,256,256]{2,1,0:T(8,128)(2,1)S(1)} %get-tuple-element.50), channel_id=1, source_target_pairs={{0,112},{1,48},{16,96},{17,32},{32,80},{33,16},{48,64},{49,0},{64,... | collective-permute-start | bytes 786440 | tf_op jit(solution)/shard_map/ppermute | solution.py:328
  83.2 13.8 %collective-permute-start.4 = (bf16[2,256,256]{2,1,0:T(8,128)(2,1)S(1)}, bf16[2,256,256]{2,1,0:T(8,128)(2,1)S(1)}, u32[]{:S(2)}, u32[]{:S(2)}) collective-permute-start(bf16[2,256,256]{2,1,0:T(8,128)(2,1)S(1)} %get-tuple-element.44), channel_id=1, source_target_pairs={{0,0},{1,64},{16,16},{17,80},{32,32},{33,96},{48,48},{49,112},{64,... | collective-permute-start | bytes 786440 | tf_op jit(solution)/shard_map/ppermute | solution.py:328
  86.3 10.7 %collective-permute-start.5 = (bf16[2,256,256]{2,1,0:T(8,128)(2,1)S(1)}, bf16[2,256,256]{2,1,0:T(8,128)(2,1)S(1)}, u32[]{:S(2)}, u32[]{:S(2)}) collective-permute-start(bf16[2,256,256]{2,1,0:T(8,128)(2,1)S(1)} %get-tuple-element.45), channel_id=1, source_target_pairs={{0,64},{1,0},{16,80},{17,16},{32,96},{33,32},{48,112},{49,48},{64,... | collective-permute-start | bytes 786440 | tf_op jit(solution)/shard_map/ppermute | solution.py:328

commit v4 on v3

--- a/solution.py
+++ b/solution.py
@@ -15,14 +15,14 @@
 TAPS = 64
 ROUNDS = 2
 STEP_WINDOWS = 8
-FIRST_PARTS = 4
+FIRST_PARTS = 1
 PIECES = 3
 TILE = 16
 VMEM = 32 * 1024 * 1024
 SMALL_VMEM = 8 * 1024 * 1024
 FIRST = 2
-CALLS = ((6, 4, 3), (7, 5, 0, 1))
-JOINED_EARLY = 5
+CALLS = ((6, 4, 3), (7, 5), (0, 1))
+JOINED_LAST = (5, 0, 1)
 
 
 def dft_rows(chips, blocks):
@@ -92,12 +92,8 @@
     )(*(pltpu.with_memory_space_constraint(given, pltpu.HBM) for given in (fir_taps, dft)))
 
 
-NT = (((1,), (1,)), ((), ()))
-
-
-def last_samples(samples):
-    end = samples[:, samples.shape[1] - TAPS :]
-    return jnp.concatenate([end] * (WL // TAPS), axis=1)
+def last_samples(across):
+    return jnp.concatenate([across[across.shape[0] - TAPS :]] * (WL // TAPS), axis=0)
 
 
 def spectra_kernel(
@@ -142,12 +138,10 @@
         for inner in range(STEP_WINDOWS):
             if isinstance(group, int) and inner * WL % first == 0:
                 fetch_first(inner * WL // first).wait()
-            samples = samples_ref[group, :, inner * WL : (inner + 1) * WL]
-            rows = lax.dot_general(main_ref[...], samples, NT, preferred_element_type=jnp.float32)
+            across = samples_ref[group, :, inner * WL : (inner + 1) * WL].T
+            rows = jnp.dot(main_ref[...], across, preferred_element_type=jnp.float32)
             stacked = rows[2 * count :] + rows[count : 2 * count] + carry + rows[:count]
-            carry = lax.dot_general(
-                before, last_samples(samples), NT, preferred_element_type=jnp.float32
-            )
+            carry = jnp.dot(before, last_samples(across), preferred_element_type=jnp.float32)
             power = jnp.sum(stacked * stacked, axis=0, keepdims=True) * (1.0 / count) + 1e-06
             held_ref[inner] = (stacked * (1.0 / jnp.sqrt(power))).astype(jnp.bfloat16)
         carry_ref[...] = carry
@@ -168,9 +162,7 @@
         fetch_first(part).start()
     for group in range(1, groups):
         fetch(group).start()
-    carry_ref[...] = lax.dot_general(
-        before, last_samples(tail_ref[...]), NT, preferred_element_type=jnp.float32
-    )
+    carry_ref[...] = jnp.dot(before, last_samples(tail_ref[...].T), preferred_element_type=jnp.float32)
     make(0)
 
     @pl.loop(1, groups)
@@ -312,7 +304,6 @@
     here, first_other = lax.optimization_barrier((here, first_other))
     other = lax.ppermute(here, "core", swap)
     parts = []
-    last = ()
     for call in ((FIRST,), *CALLS):
         products = cross(call, plan, place, here, first_other if call == (FIRST,) else other, scale)
         if call == (FIRST,):
@@ -327,9 +318,12 @@
             ]
             parts.append(lax.ppermute(product, ("chan", "core"), route))
     steps = [FIRST] + [step for call in CALLS for step in call]
-    if JOINED_EARLY:
-        last = [join(steps[:JOINED_EARLY], place, parts[:JOINED_EARLY], half)]
-    return join(steps[JOINED_EARLY:], place, parts[JOINED_EARLY:], half, last)
+    arrived = dict(zip(steps, parts))
+    done = ()
+    for late in (False, True):
+        now = [step for step in steps if (step in JOINED_LAST) == late]
+        done = [join(now, place, [arrived[step] for step in now], half, done)]
+    return done[0]
 
 
 def solution(mesh):

time: 99.1 us -> 97.6 us (0.985)
    pallas_call x1, Pallas kernels: 8.25 us -> 6.91 us  [spectra(): pl.pallas_call(spectra_kernel, out_shape=pltpu.HBM(result, jnp.bfloat16),...]
    ppermute x8, waiting for transfers between devices: 7.06 us -> 5.73 us  [on_device(): parts.append(lax.ppermute(product, ('chan', 'core'), route))]
    pallas_call x3 -> x4, Pallas kernels: 4.96 us -> 5.71 us  [cross(): pl.pallas_call(functools.partial(cross_kernel, scale, steps), in_specs=[I...]
  transfers between devices with their start and end apart: 12 -> 12, of which waited for: 7 -> 5; matrix products, arithmetic and copies ran while one was open for 1% -> 1% of each run, Pallas kernels for 9% -> 9%
where the time goes in v4:
time: 97.6 us; the launch traced here: 97.3 us
  waiting for transfers between devices  38.4 us (39%)
  starting transfers between devices  37.5 us (38%)
  Pallas kernels  17.9 us (18%)
  between operations  1.87 us (2%)
  local copies, waits for them, and re-layouts  1.48 us (2%)
    all_to_all x1, waiting for transfers between devices, on_device(): here = lax.all_to_all(white, ('chan', 'chip'), 0, 0, tiled=True)  30.6 us
    ppermute x8, starting transfers between devices, on_device(): parts.append(lax.ppermute(product, ('chan', 'core'), route))  17.8 us
    all_to_all x1, starting transfers between devices, on_device(): here = lax.all_to_all(white, ('chan', 'chip'), 0, 0, tiled=True)  10.8 us
    pallas_call x1, Pallas kernels, spectra(): pl.pallas_call(spectra_kernel, out_shape=pltpu.HBM(result, jnp.bfloat16),...  6.91 us
    ppermute x8, waiting for transfers between devices, on_device(): parts.append(lax.ppermute(product, ('chan', 'core'), route))  5.73 us
    pallas_call x4, Pallas kernels, cross(): pl.pallas_call(functools.partial(cross_kernel, scale, steps), in_specs=[I...  5.71 us
    ppermute x1, starting transfers between devices, on_device(): lax.ppermute(records[:, samples_here - WL // 2:], ('chip', 'core'), [(i,...  4.58 us
    ppermute x1, starting transfers between devices, on_device(): first_other = lax.ppermute(jnp.stack(away), 'core', swap)  3.96 us
  transfers between devices with their start and end apart: 12, of which 5 were waited for; matrix products, arithmetic and copies ran while one was open for 1% of the time, Pallas kernels for 9%

profile of v4, /device:TPU:1, one launch (start us, length us, event | category | flops | bytes accessed | tf_op | source)
XLA Modules:
  0.0 97.3 jit_solution(14797803367715574767)
XLA Ops:
  0.0 0.8 slice.3
  0.8 4.6 %collective-permute-start = (bf16[256,128]{1,0:T(8,128)(2,1)S(1)}, bf16[256,128]{1,0:T(8,128)(2,1)S(1)}, u32[]{:S(2)}, u32[]{:S(2)}) collective-permute-start(bf16[256,128]{1,0:T(8,128)(2,1)S(1)} %slice.3), channel_id=1, source_target_pairs={{0,1},{1,2},{2,3},{3,4},{4,5},{5,6},{6,7},{7,8},{8,9},{9,10},{10,1... | collective-permute-start | bytes 196616 | tf_op jit(solution)/shard_map/ppermute | solution.py:291
  5.4 1.4 %table.1 = (bf16[384,256]{1,0:T(8,128)(2,1)S(1)}, bf16[128,256]{1,0:T(8,128)(2,1)S(1)}, bf16[256,256]{1,0:T(8,128)(2,1)S(1)}) custom-call(f32[64]{0:T(128)} %taps_at.1, f32[128,256]{1,0:T(8,128)} %constant.23.clone.dft_at), custom_call_target="tpu_custom_call" | custom-call | tf_op jit(solution)/shard_map/table/pallas_call | solution.py:80
  6.9 6.9 %spectra.1 = bf16[64,80,256]{2,1,0:T(8,128)(2,1)} custom-call(bf16[256,128]{1,0:T(8,128)(2,1)S(1)} %collective-permute-done.tail_ref, bf16[384,256]{1,0:T(8,128)(2,1)S(1)} %get-tuple-element.30.main_ref, bf16[128,256]{1,0:T(8,128)(2,1)S(1)} %get-tuple-element.31.before_ref, bf16[256,256]{1,0:T(8,128)(2,1)S(1)} %get-tuple-element.32.order_ref, ...), custom_call_target="tpu_custom_call" | custom-call | tf_op jit(solution)/shard_map/spectra/pallas_call | solution.py:185
  13.8 10.8 %all-to-all-start = ((bf16[64,80,256]{2,1,0:T(8,128)(2,1)}), bf16[64,80,256]{2,1,0:T(8,128)(2,1)S(1)}, u32[]{:S(2)}, u32[]{:S(2)}) async-start(bf16[64,80,256]{2,1,0:T(8,128)(2,1)} %spectra.1), calls=%async_computation | async-start | bytes 5242880 | tf_op jit(solution)/shard_map/all_to_all | solution.py:297
  26.9 30.6 %all-to-all-done = bf16[64,80,256]{2,1,0:T(8,128)(2,1)S(1)} async-done(((bf16[64,80,256]{2,1,0:T(8,128)(2,1)}), bf16[64,80,256]{2,1,0:T(8,128)(2,1)S(1)}, u32[]{:S(2)}, u32[]{:S(2)}) %all-to-all-start) | async-done | bytes 2621472 | tf_op jit(solution)/shard_map/all_to_all | solution.py:297
  57.7 4.0 %collective-permute-start.1 = (bf16[2,640,256]{2,1,0:T(8,128)(2,1)S(1)}, bf16[2,640,256]{2,1,0:T(8,128)(2,1)S(1)}, u32[]{:S(2)}, u32[]{:S(2)}) collective-permute-start(bf16[2,640,256]{2,1,0:T(8,128)(2,1)S(1)} %pad_maximum_fusion), channel_id=1, source_target_pairs={{0,1},{1,0},{2,3},{3,2},{4,5},{5,4},{6,7},{7,6},{8,9},{9,8},{10,11... | collective-permute-start | bytes 1966088 | tf_op jit(solution)/shard_map/ppermute | solution.py:303
  61.6 1.7 %collective-permute-done.1.other_ref = bf16[2,640,256]{2,1,0:T(8,128)(2,1)S(1)} collective-permute-done((bf16[2,640,256]{2,1,0:T(8,128)(2,1)S(1)}, bf16[2,640,256]{2,1,0:T(8,128)(2,1)S(1)}, u32[]{:S(2)}, u32[]{:S(2)}) %collective-permute-start.1) | collective-permute-done | bytes 655392 | tf_op jit(solution)/shard_map/ppermute | solution.py:303
  63.8 1.1 %cross.4 = bf16[2,256,256]{2,1,0:T(8,128)(2,1)S(1)} custom-call(s32[2,8]{1,0:T(2,128)S(1)} %copy-done, s32[2]{0:T(128)S(1)} %pad_add_fusion.place_ref, bf16[8,640,256]{2,1,0:T(8,128)(2,1)S(1)} %bitcast.6, bf16[2,640,256]{2,1,0:T(8,128)(2,1)S(1)} %collective-permute-done.1.other_ref), custom_call_target="tpu_custom_call" | custom-call | flops 335544320 | bytes 1572864 | tf_op jit(solution)/shard_map/cross/pallas_call | solution.py:235
  64.9 3.0 %collective-permute-start.6 = (bf16[2,256,256]{2,1,0:T(8,128)(2,1)S(1)}, bf16[2,256,256]{2,1,0:T(8,128)(2,1)S(1)}, u32[]{:S(2)}, u32[]{:S(2)}) collective-permute-start(bf16[2,256,256]{2,1,0:T(8,128)(2,1)S(1)} %cross.4), channel_id=1, source_target_pairs={{0,16},{1,80},{16,0},{17,64},{32,48},{33,112},{48,32},{49,96},{64,... | collective-permute-start | bytes 786440 | tf_op jit(solution)/shard_map/ppermute | solution.py:319
  68.3 1.8 %cross.5 = (bf16[2,256,256]{2,1,0:T(8,128)(2,1)S(1)}, bf16[2,256,256]{2,1,0:T(8,128)(2,1)S(1)}, bf16[2,256,256]{2,1,0:T(8,128)(2,1)S(1)}) custom-call(s32[2,8]{1,0:T(2,128)S(1)} %copy-done, s32[2]{0:T(128)S(1)} %pad_add_fusion.place_ref, bf16[8,640,256]{2,1,0:T(8,128)(2,1)S(1)} %bitcast.7, bf16[8,640,256]{2,1,0:T(8,128)(2,1)S(1)} %collective-permute-done.2.other_ref), custom_call_target="tpu_custom_call" | custom-call | flops 1006632960 | bytes 4718592 | tf_op jit(solution)/shard_map/cross/pallas_call | solution.py:235
  70.0 1.3 %collective-permute-start.7 = (bf16[2,256,256]{2,1,0:T(8,128)(2,1)S(1)}, bf16[2,256,256]{2,1,0:T(8,128)(2,1)S(1)}, u32[]{:S(2)}, u32[]{:S(2)}) collective-permute-start(bf16[2,256,256]{2,1,0:T(8,128)(2,1)S(1)} %get-tuple-element.51), channel_id=1, source_target_pairs={{0,48},{1,112},{16,32},{17,96},{32,16},{33,80},{48,0},{49,64},{64,... | collective-permute-start | bytes 786440 | tf_op jit(solution)/shard_map/ppermute | solution.py:319
  71.3 2.3 %collective-permute-start.8 = (bf16[2,256,256]{2,1,0:T(8,128)(2,1)S(1)}, bf16[2,256,256]{2,1,0:T(8,128)(2,1)S(1)}, u32[]{:S(2)}, u32[]{:S(2)}) collective-permute-start(bf16[2,256,256]{2,1,0:T(8,128)(2,1)S(1)} %get-tuple-element.52), channel_id=1, source_target_pairs={{0,32},{1,96},{16,48},{17,112},{32,0},{33,64},{48,16},{49,80},{64,... | collective-permute-start | bytes 786440 | tf_op jit(solution)/shard_map/ppermute | solution.py:319
  73.6 1.4 %collective-permute-start.9 = (bf16[2,256,256]{2,1,0:T(8,128)(2,1)S(1)}, bf16[2,256,256]{2,1,0:T(8,128)(2,1)S(1)}, u32[]{:S(2)}, u32[]{:S(2)}) collective-permute-start(bf16[2,256,256]{2,1,0:T(8,128)(2,1)S(1)} %get-tuple-element.53), channel_id=1, source_target_pairs={{0,80},{1,16},{16,64},{17,0},{32,112},{33,48},{48,96},{49,32},{64,... | collective-permute-start | bytes 786440 | tf_op jit(solution)/shard_map/ppermute | solution.py:319
  75.1 1.4 %cross.6 = (bf16[2,256,256]{2,1,0:T(8,128)(2,1)S(1)}, bf16[2,256,256]{2,1,0:T(8,128)(2,1)S(1)}) custom-call(s32[2,8]{1,0:T(2,128)S(1)} %copy-done, s32[2]{0:T(128)S(1)} %pad_add_fusion.place_ref, bf16[8,640,256]{2,1,0:T(8,128)(2,1)S(1)} %bitcast.8, bf16[8,640,256]{2,1,0:T(8,128)(2,1)S(1)} %collective-permute-done.2.other_ref), custom_call_target="tpu_custom_call" | custom-call | flops 671088640 | bytes 3145728 | tf_op jit(solution)/shard_map/cross/pallas_call | solution.py:235
  76.5 0.9 collective-permute-start.3
  77.4 1.4 %cross.7 = (bf16[2,256,256]{2,1,0:T(8,128)(2,1)S(1)}, bf16[2,256,256]{2,1,0:T(8,128)(2,1)S(1)}) custom-call(s32[2,8]{1,0:T(2,128)S(1)} %copy-done, s32[2]{0:T(128)S(1)} %pad_add_fusion.place_ref, bf16[8,640,256]{2,1,0:T(8,128)(2,1)S(1)} %bitcast.9, bf16[8,640,256]{2,1,0:T(8,128)(2,1)S(1)} %collective-permute-done.2.other_ref), custom_call_target="tpu_custom_call" | custom-call | flops 671088640 | bytes 3145728 | tf_op jit(solution)/shard_map/cross/pallas_call | solution.py:235
  78.9 3.4 %collective-permute-start.10 = (bf16[2,256,256]{2,1,0:T(8,128)(2,1)S(1)}, bf16[2,256,256]{2,1,0:T(8,128)(2,1)S(1)}, u32[]{:S(2)}, u32[]{:S(2)}) collective-permute-start(bf16[2,256,256]{2,1,0:T(8,128)(2,1)S(1)} %get-tuple-element.54), channel_id=1, source_target_pairs={{0,112},{1,48},{16,96},{17,32},{32,80},{33,16},{48,64},{49,0},{64,... | collective-permute-start | bytes 786440 | tf_op jit(solution)/shard_map/ppermute | solution.py:319
  82.3 3.5 %collective-permute-start.4 = (bf16[2,256,256]{2,1,0:T(8,128)(2,1)S(1)}, bf16[2,256,256]{2,1,0:T(8,128)(2,1)S(1)}, u32[]{:S(2)}, u32[]{:S(2)}) collective-permute-start(bf16[2,256,256]{2,1,0:T(8,128)(2,1)S(1)} %get-tuple-element.48), channel_id=1, source_target_pairs={{0,0},{1,64},{16,16},{17,80},{32,32},{33,96},{48,48},{49,112},{64,... | collective-permute-start | bytes 786440 | tf_op jit(solution)/shard_map/ppermute | solution.py:319
  85.8 1.9 %collective-permute-start.5 = (bf16[2,256,256]{2,1,0:T(8,128)(2,1)S(1)}, bf16[2,256,256]{2,1,0:T(8,128)(2,1)S(1)}, u32[]{:S(2)}, u32[]{:S(2)}) collective-permute-start(bf16[2,256,256]{2,1,0:T(8,128)(2,1)S(1)} %get-tuple-element.49), channel_id=1, source_target_pairs={{0,64},{1,0},{16,80},{17,16},{32,96},{33,32},{48,112},{49,48},{64,... | collective-permute-start | bytes 786440 | tf_op jit(solution)/shard_map/ppermute | solution.py:319
  87.7 3.7 %collective-permute-done.10.refs_4_ = bf16[2,256,256]{2,1,0:T(8,128)(2,1)S(1)} collective-permute-done((bf16[2,256,256]{2,1,0:T(8,128)(2,1)S(1)}, bf16[2,256,256]{2,1,0:T(8,128)(2,1)S(1)}, u32[]{:S(2)}, u32[]{:S(2)}) %collective-permute-start.10) | collective-permute-done | bytes 262176 | tf_op jit(solution)/shard_map/ppermute | solution.py:319
  91.4 2.1 %join.2.refs_3_ = f32[4,2,2,256,256]{4,3,2,1,0:T(8,128)} custom-call(s32[2]{0:T(128)S(1)} %pad_add_fusion.place_ref, bf16[2,256,256]{2,1,0:T(8,128)(2,1)S(1)} %collective-permute-done.6.refs_0_, bf16[2,256,256]{2,1,0:T(8,128)(2,1)S(1)} %collective-permute-done.7.refs_1_, bf16[2,256,256]{2,1,0:T(8,128)(2,1)S(1)} %collective-permute-done.8.refs_2_, ...), custom_call_target="tpu_custom_call" | custom-call | bytes 3932160 | tf_op jit(solution)/shard_map/join/pallas_call | solution.py:266
  93.6 2.0 %collective-permute-done.5.refs_2_ = bf16[2,256,256]{2,1,0:T(8,128)(2,1)S(1)} collective-permute-done((bf16[2,256,256]{2,1,0:T(8,128)(2,1)S(1)}, bf16[2,256,256]{2,1,0:T(8,128)(2,1)S(1)}, u32[]{:S(2)}, u32[]{:S(2)}) %collective-permute-start.5) | collective-permute-done | bytes 262176 | tf_op jit(solution)/shard_map/ppermute | solution.py:319
  95.6 1.7 %join.3 = f32[4,2,2,256,256]{4,3,2,1,0:T(8,128)} custom-call(s32[2]{0:T(128)S(1)} %pad_add_fusion.place_ref, bf16[2,256,256]{2,1,0:T(8,128)(2,1)S(1)} %collective-permute-done.3.refs_0_, bf16[2,256,256]{2,1,0:T(8,128)(2,1)S(1)} %collective-permute-done.4.refs_1_, ...), custom_call_target="tpu_custom_call", output_to_operand_aliasing={{}: (4, {})} | custom-call | bytes 2359296 | tf_op jit(solution)/shard_map/join/pallas_call | solution.py:266
  (15 shorter events, 1.5 us)
Async XLA Ops:
  0.8 6.0 %collective-permute-start = (bf16[256,128]{1,0:T(8,128)(2,1)S(1)}, bf16[256,128]{1,0:T(8,128)(2,1)S(1)}, u32[]{:S(2)}, u32[]{:S(2)}) collective-permute-start(bf16[256,128]{1,0:T(8,128)(2,1)S(1)} %slice.3), channel_id=1, source_target_pairs={{0,1},{1,2},{2,3},{3,4},{4,5},{5,6},{6,7},{7,8},{8,9},{9,10},{10,1... | collective-permute-start | bytes 196616 | tf_op jit(solution)/shard_map/ppermute | solution.py:291
  13.8 10.9 %copy-start = (s32[2,8]{1,0:T(2,128)S(1)}, s32[2,8]{1,0:T(2,128)}, u32[]{:S(2)}) copy-start(s32[2,8]{1,0:T(2,128)} %plan_ref.7) | copy-start | bytes 196
  13.8 43.7 %all-to-all-start = ((bf16[64,80,256]{2,1,0:T(8,128)(2,1)}), bf16[64,80,256]{2,1,0:T(8,128)(2,1)S(1)}, u32[]{:S(2)}, u32[]{:S(2)}) async-start(bf16[64,80,256]{2,1,0:T(8,128)(2,1)} %spectra.1), calls=%async_computation | async-start | bytes 5242880 | tf_op jit(solution)/shard_map/all_to_all | solution.py:297
  57.7 5.7 %collective-permute-start.1 = (bf16[2,640,256]{2,1,0:T(8,128)(2,1)S(1)}, bf16[2,640,256]{2,1,0:T(8,128)(2,1)S(1)}, u32[]{:S(2)}, u32[]{:S(2)}) collective-permute-start(bf16[2,640,256]{2,1,0:T(8,128)(2,1)S(1)} %pad_maximum_fusion), channel_id=1, source_target_pairs={{0,1},{1,0},{2,3},{3,2},{4,5},{5,4},{6,7},{7,6},{8,9},{9,8},{10,11... | collective-permute-start | bytes 1966088 | tf_op jit(solution)/shard_map/ppermute | solution.py:303
  63.4 4.9 %collective-permute-start.2 = (bf16[8,640,256]{2,1,0:T(8,128)(2,1)S(1)}, bf16[8,640,256]{2,1,0:T(8,128)(2,1)S(1)}, u32[]{:S(2)}, u32[]{:S(2)}) collective-permute-start(bf16[8,640,256]{2,1,0:T(8,128)(2,1)S(1)} %bitcast.5), channel_id=1, source_target_pairs={{0,1},{1,0},{2,3},{3,2},{4,5},{5,4},{6,7},{7,6},{8,9},{9,8},{10,11... | collective-permute-start | bytes 7864328 | tf_op jit(solution)/shard_map/ppermute | solution.py:305
  64.9 14.0 %collective-permute-start.6 = (bf16[2,256,256]{2,1,0:T(8,128)(2,1)S(1)}, bf16[2,256,256]{2,1,0:T(8,128)(2,1)S(1)}, u32[]{:S(2)}, u32[]{:S(2)}) collective-permute-start(bf16[2,256,256]{2,1,0:T(8,128)(2,1)S(1)} %cross.4), channel_id=1, source_target_pairs={{0,16},{1,80},{16,0},{17,64},{32,48},{33,112},{48,32},{49,96},{64,... | collective-permute-start | bytes 786440 | tf_op jit(solution)/shard_map/ppermute | solution.py:319
  70.0 12.3 %collective-permute-start.7 = (bf16[2,256,256]{2,1,0:T(8,128)(2,1)S(1)}, bf16[2,256,256]{2,1,0:T(8,128)(2,1)S(1)}, u32[]{:S(2)}, u32[]{:S(2)}) collective-permute-start(bf16[2,256,256]{2,1,0:T(8,128)(2,1)S(1)} %get-tuple-element.51), channel_id=1, source_target_pairs={{0,48},{1,112},{16,32},{17,96},{32,16},{33,80},{48,0},{49,64},{64,... | collective-permute-start | bytes 786440 | tf_op jit(solution)/shard_map/ppermute | solution.py:319
  71.3 14.4 %collective-permute-start.8 = (bf16[2,256,256]{2,1,0:T(8,128)(2,1)S(1)}, bf16[2,256,256]{2,1,0:T(8,128)(2,1)S(1)}, u32[]{:S(2)}, u32[]{:S(2)}) collective-permute-start(bf16[2,256,256]{2,1,0:T(8,128)(2,1)S(1)} %get-tuple-element.52), channel_id=1, source_target_pairs={{0,32},{1,96},{16,48},{17,112},{32,0},{33,64},{48,16},{49,80},{64,... | collective-permute-start | bytes 786440 | tf_op jit(solution)/shard_map/ppermute | solution.py:319
  73.6 14.1 %collective-permute-start.9 = (bf16[2,256,256]{2,1,0:T(8,128)(2,1)S(1)}, bf16[2,256,256]{2,1,0:T(8,128)(2,1)S(1)}, u32[]{:S(2)}, u32[]{:S(2)}) collective-permute-start(bf16[2,256,256]{2,1,0:T(8,128)(2,1)S(1)} %get-tuple-element.53), channel_id=1, source_target_pairs={{0,80},{1,16},{16,64},{17,0},{32,112},{33,48},{48,96},{49,32},{64,... | collective-permute-start | bytes 786440 | tf_op jit(solution)/shard_map/ppermute | solution.py:319
  76.5 17.0 %collective-permute-start.3 = (bf16[2,256,256]{2,1,0:T(8,128)(2,1)S(1)}, bf16[2,256,256]{2,1,0:T(8,128)(2,1)S(1)}, u32[]{:S(2)}, u32[]{:S(2)}) collective-permute-start(bf16[2,256,256]{2,1,0:T(8,128)(2,1)S(1)} %get-tuple-element.43), channel_id=1, source_target_pairs={{0,96},{1,32},{16,112},{17,48},{32,64},{33,0},{48,80},{49,16},{64,... | collective-permute-start | bytes 786440 | tf_op jit(solution)/shard_map/ppermute | solution.py:319
  78.9 12.5 %collective-permute-start.10 = (bf16[2,256,256]{2,1,0:T(8,128)(2,1)S(1)}, bf16[2,256,256]{2,1,0:T(8,128)(2,1)S(1)}, u32[]{:S(2)}, u32[]{:S(2)}) collective-permute-start(bf16[2,256,256]{2,1,0:T(8,128)(2,1)S(1)} %get-tuple-element.54), channel_id=1, source_target_pairs={{0,112},{1,48},{16,96},{17,32},{32,80},{33,16},{48,64},{49,0},{64,... | collective-permute-start | bytes 786440 | tf_op jit(solution)/shard_map/ppermute | solution.py:319
  82.3 11.2 %collective-permute-start.4 = (bf16[2,256,256]{2,1,0:T(8,128)(2,1)S(1)}, bf16[2,256,256]{2,1,0:T(8,128)(2,1)S(1)}, u32[]{:S(2)}, u32[]{:S(2)}) collective-permute-start(bf16[2,256,256]{2,1,0:T(8,128)(2,1)S(1)} %get-tuple-element.48), channel_id=1, source_target_pairs={{0,0},{1,64},{16,16},{17,80},{32,32},{33,96},{48,48},{49,112},{64,... | collective-permute-start | bytes 786440 | tf_op jit(solution)/shard_map/ppermute | solution.py:319
  85.8 9.8 %collective-permute-start.5 = (bf16[2,256,256]{2,1,0:T(8,128)(2,1)S(1)}, bf16[2,256,256]{2,1,0:T(8,128)(2,1)S(1)}, u32[]{:S(2)}, u32[]{:S(2)}) collective-permute-start(bf16[2,256,256]{2,1,0:T(8,128)(2,1)S(1)} %get-tuple-element.49), channel_id=1, source_target_pairs={{0,64},{1,0},{16,80},{17,16},{32,96},{33,32},{48,112},{49,48},{64,... | collective-permute-start | bytes 786440 | tf_op jit(solution)/shard_map/ppermute | solution.py:319

commit v5 on v4

--- a/solution.py
+++ b/solution.py
@@ -15,7 +15,6 @@
 TAPS = 64
 ROUNDS = 2
 STEP_WINDOWS = 8
-FIRST_PARTS = 1
 PIECES = 3
 TILE = 16
 VMEM = 32 * 1024 * 1024
@@ -42,11 +41,17 @@
     return pieces
 
 
-def table_kernel(taps_at, dft_at, main_ref, before_ref, order_ref, taps_ref, dft_ref, sems):
+def table_kernel(
+    taps_at, dft_at, records_ref, main_ref, before_ref, order_ref, early_ref, taps_ref, dft_ref, sems
+):
     taps_copy = pltpu.make_async_copy(taps_at, taps_ref, sems.at[0])
     dft_copy = pltpu.make_async_copy(dft_at, dft_ref, sems.at[1])
     taps_copy.start()
     dft_copy.start()
+    early_copy = pltpu.make_async_copy(
+        records_ref.at[:, : STEP_WINDOWS * WL], early_ref, sems.at[2]
+    )
+    early_copy.start()
     row = lax.broadcasted_iota(jnp.int32, order_ref.shape, 0)
     column = lax.broadcasted_iota(jnp.int32, order_ref.shape, 1)
     source = (row & 7) * 32 + ((row >> 3) & 1) * 16 + (row >> 4)
@@ -68,6 +73,7 @@
     first = jnp.where(left, pltpu.roll(high, TAPS, 1), middle)
     second = jnp.where(left, pltpu.roll(low, TAPS, 1), 0.0)
     before_ref[...] = jnp.concatenate([first, second], axis=1).astype(jnp.bfloat16)
+    early_copy.wait()
 
 
 IN_VMEM = pl.BlockSpec(memory_space=pltpu.VMEM)
@@ -75,21 +81,22 @@
 IN_HBM = pl.BlockSpec(memory_space=pltpu.HBM)
 
 
-def make_tables(fir_taps, dft):
+def make_tables(fir_taps, dft, records):
     rows = (PIECES * 2 * F, 2 * F, WL)
     return pl.pallas_call(
         table_kernel,
-        out_shape=[jax.ShapeDtypeStruct((count, WL), jnp.bfloat16) for count in rows],
-        in_specs=[IN_HBM, IN_HBM],
-        out_specs=[IN_VMEM] * 3,
+        out_shape=[jax.ShapeDtypeStruct((count, WL), jnp.bfloat16) for count in rows]
+        + [jax.ShapeDtypeStruct((records.shape[0], STEP_WINDOWS * WL), jnp.bfloat16)],
+        in_specs=[IN_HBM] * 3,
+        out_specs=[IN_VMEM] * 4,
         scratch_shapes=[
             pltpu.SMEM(fir_taps.shape, jnp.float32),
             pltpu.VMEM(dft.shape, jnp.float32),
-            pltpu.SemaphoreType.DMA((2,)),
+            pltpu.SemaphoreType.DMA((3,)),
         ],
         compiler_params=pltpu.CompilerParams(vmem_limit_bytes=SMALL_VMEM),
         name="table",
-    )(*(pltpu.with_memory_space_constraint(given, pltpu.HBM) for given in (fir_taps, dft)))
+    )(*(pltpu.with_memory_space_constraint(given, pltpu.HBM) for given in (fir_taps, dft, records)))
 
 
 def last_samples(across):
@@ -101,6 +108,7 @@
     main_ref,
     before_ref,
     order_ref,
+    early_ref,
     records_ref,
     out_ref,
     samples_ref,
@@ -110,21 +118,14 @@
     in_sems,
     out_sems,
 ):
-    groups = samples_ref.shape[0]
+    groups = samples_ref.shape[0] + 1
     width = STEP_WINDOWS * WL
-    first = width // FIRST_PARTS
     count = 2 * F
     before = before_ref[...]
 
-    def fetch_first(part):
-        lanes = pl.ds(part * first, first)
-        return pltpu.make_async_copy(
-            records_ref.at[:, lanes], samples_ref.at[0, :, lanes], in_sems.at[groups + part]
-        )
-
     def fetch(group):
         source = records_ref.at[:, pl.ds(pl.multiple_of(group * width, width), width)]
-        return pltpu.make_async_copy(source, samples_ref.at[group], in_sems.at[group])
+        return pltpu.make_async_copy(source, samples_ref.at[group - 1], in_sems.at[group - 1])
 
     def rows_of(group):
         return pl.ds(pl.multiple_of(group * TILE, TILE), TILE)
@@ -133,12 +134,10 @@
         at = rows_of(group)
         return pltpu.make_async_copy(white_ref.at[:, at, :], out_ref.at[:, at, :], out_sems.at[group])
 
-    def make(group):
+    def make(samples_at):
         carry = carry_ref[...]
         for inner in range(STEP_WINDOWS):
-            if isinstance(group, int) and inner * WL % first == 0:
-                fetch_first(inner * WL // first).wait()
-            across = samples_ref[group, :, inner * WL : (inner + 1) * WL].T
+            across = samples_at[:, inner * WL : (inner + 1) * WL].T
             rows = jnp.dot(main_ref[...], across, preferred_element_type=jnp.float32)
             stacked = rows[2 * count :] + rows[count : 2 * count] + carry + rows[:count]
             carry = jnp.dot(before, last_samples(across), preferred_element_type=jnp.float32)
@@ -158,18 +157,16 @@
             for n in range(TILE):
                 white_ref[part * TILE + n, rows_of(group), :] = placed[n * TILE : (n + 1) * TILE]
 
-    for part in range(FIRST_PARTS):
-        fetch_first(part).start()
     for group in range(1, groups):
         fetch(group).start()
     carry_ref[...] = jnp.dot(before, last_samples(tail_ref[...].T), preferred_element_type=jnp.float32)
-    make(0)
+    make(early_ref)
 
     @pl.loop(1, groups)
     def _(group):
         fetch(group).wait()
         place(group - 1)
-        make(group)
+        make(samples_ref.at[group - 1])
         send(group - 1).start()
 
     place(groups - 1)
@@ -185,14 +182,14 @@
     return pl.pallas_call(
         spectra_kernel,
         out_shape=pltpu.HBM(result, jnp.bfloat16),
-        in_specs=[IN_VMEM] * 4 + [IN_HBM],
+        in_specs=[IN_VMEM] * 5 + [IN_HBM],
         out_specs=IN_HBM,
         scratch_shapes=[
-            pltpu.VMEM((groups, channels, STEP_WINDOWS * WL), jnp.bfloat16),
+            pltpu.VMEM((groups - 1, channels, STEP_WINDOWS * WL), jnp.bfloat16),
             pltpu.VMEM((2 * F, channels), jnp.float32),
             pltpu.VMEM((STEP_WINDOWS, 2 * F, channels), jnp.bfloat16),
             pltpu.VMEM(result, jnp.bfloat16),
-            pltpu.SemaphoreType.DMA((groups + FIRST_PARTS,)),
+            pltpu.SemaphoreType.DMA((groups - 1,)),
             pltpu.SemaphoreType.DMA((groups,)),
         ],
         compiler_params=pltpu.CompilerParams(vmem_limit_bytes=VMEM),
@@ -293,7 +290,7 @@
     )
     swap = [(0, 1), (1, 0)]
     scale = 1.0 / math.sqrt(samples_here // WL * count)
-    white = spectra(tail, make_tables(fir_taps, dft), records)
+    white = spectra(tail, make_tables(fir_taps, dft, records), records)
     here = lax.all_to_all(white, ("chan", "chip"), 0, 0, tiled=True)
     here = here.reshape(blocks, chips * white.shape[1], channels)
     half = blocks // 2

time: 97.6 us -> 96.9 us (level)
  transfers between devices with their start and end apart: 12 -> 12, of which waited for: 5 -> 5; matrix products, arithmetic and copies ran while one was open for 1% -> 1% of each run, Pallas kernels for 9% -> 10%
where the time goes in v5:
time: 96.9 us; the launch traced here: 96.5 us
  waiting for transfers between devices  38.5 us (40%)
  starting transfers between devices  37.5 us (39%)
  Pallas kernels  17.1 us (18%)
  between operations  1.87 us (2%)
  local copies, waits for them, and re-layouts  1.48 us (2%)
    all_to_all x1, waiting for transfers between devices, on_device(): here = lax.all_to_all(white, ('chan', 'chip'), 0, 0, tiled=True)  30.6 us
    ppermute x8, starting transfers between devices, on_device(): parts.append(lax.ppermute(product, ('chan', 'core'), route))  17.7 us
    all_to_all x1, starting transfers between devices, on_device(): here = lax.all_to_all(white, ('chan', 'chip'), 0, 0, tiled=True)  10.9 us
    pallas_call x1, Pallas kernels, spectra(): pl.pallas_call(spectra_kernel, out_shape=pltpu.HBM(result, jnp.bfloat16),...  6.12 us
    ppermute x8, waiting for transfers between devices, on_device(): parts.append(lax.ppermute(product, ('chan', 'core'), route))  5.76 us
    pallas_call x4, Pallas kernels, cross(): pl.pallas_call(functools.partial(cross_kernel, scale, steps), in_specs=[I...  5.7 us
    ppermute x1, starting transfers between devices, on_device(): lax.ppermute(records[:, samples_here - WL // 2:], ('chip', 'core'), [(i,...  4.58 us
    ppermute x1, starting transfers between devices, on_device(): first_other = lax.ppermute(jnp.stack(away), 'core', swap)  3.97 us
  transfers between devices with their start and end apart: 12, of which 5 were waited for; matrix products, arithmetic and copies ran while one was open for 1% of the time, Pallas kernels for 10%

profile of v5, /device:TPU:1, one launch (start us, length us, event | category | flops | bytes accessed | tf_op | source)
XLA Modules:
  0.0 96.5 jit_solution(4055998627261379501)
XLA Ops:
  0.0 0.8 slice.3
  0.8 4.6 %collective-permute-start = (bf16[256,128]{1,0:T(8,128)(2,1)S(1)}, bf16[256,128]{1,0:T(8,128)(2,1)S(1)}, u32[]{:S(2)}, u32[]{:S(2)}) collective-permute-start(bf16[256,128]{1,0:T(8,128)(2,1)S(1)} %slice.3), channel_id=1, source_target_pairs={{0,1},{1,2},{2,3},{3,4},{4,5},{5,6},{6,7},{7,8},{8,9},{9,10},{10,1... | collective-permute-start | bytes 196616 | tf_op jit(solution)/shard_map/ppermute | solution.py:288
  5.4 1.4 %table.1 = (bf16[384,256]{1,0:T(8,128)(2,1)S(1)}, bf16[128,256]{1,0:T(8,128)(2,1)S(1)}, bf16[256,256]{1,0:T(8,128)(2,1)S(1)}, bf16[256,2048]{1,0:T(8,128)(2,1)S(1)}) custom-call(f32[64]{0:T(128)} %taps_at.1, f32[128,256]{1,0:T(8,128)} %constant.23.clone.dft_at, bf16[256,10240]{1,0:T(8,128)(2,1)} %records_ref.3), custom_call_target="tpu_custom_call" | custom-call | tf_op jit(solution)/shard_map/table/pallas_call | solution.py:86
  6.9 6.1 %spectra.1 = bf16[64,80,256]{2,1,0:T(8,128)(2,1)} custom-call(bf16[256,128]{1,0:T(8,128)(2,1)S(1)} %collective-permute-done.tail_ref, bf16[384,256]{1,0:T(8,128)(2,1)S(1)} %get-tuple-element.31.main_ref, bf16[128,256]{1,0:T(8,128)(2,1)S(1)} %get-tuple-element.32.before_ref, bf16[256,256]{1,0:T(8,128)(2,1)S(1)} %get-tuple-element.33.order_ref, ...), custom_call_target="tpu_custom_call" | custom-call | tf_op jit(solution)/shard_map/spectra/pallas_call | solution.py:182
  13.0 10.9 %all-to-all-start = ((bf16[64,80,256]{2,1,0:T(8,128)(2,1)}), bf16[64,80,256]{2,1,0:T(8,128)(2,1)S(1)}, u32[]{:S(2)}, u32[]{:S(2)}) async-start(bf16[64,80,256]{2,1,0:T(8,128)(2,1)} %spectra.1), calls=%async_computation | async-start | bytes 5242880 | tf_op jit(solution)/shard_map/all_to_all | solution.py:294
  26.2 30.6 %all-to-all-done = bf16[64,80,256]{2,1,0:T(8,128)(2,1)S(1)} async-done(((bf16[64,80,256]{2,1,0:T(8,128)(2,1)}), bf16[64,80,256]{2,1,0:T(8,128)(2,1)S(1)}, u32[]{:S(2)}, u32[]{:S(2)}) %all-to-all-start) | async-done | bytes 2621472 | tf_op jit(solution)/shard_map/all_to_all | solution.py:294
  56.9 4.0 %collective-permute-start.1 = (bf16[2,640,256]{2,1,0:T(8,128)(2,1)S(1)}, bf16[2,640,256]{2,1,0:T(8,128)(2,1)S(1)}, u32[]{:S(2)}, u32[]{:S(2)}) collective-permute-start(bf16[2,640,256]{2,1,0:T(8,128)(2,1)S(1)} %pad_maximum_fusion), channel_id=1, source_target_pairs={{0,1},{1,0},{2,3},{3,2},{4,5},{5,4},{6,7},{7,6},{8,9},{9,8},{10,11... | collective-permute-start | bytes 1966088 | tf_op jit(solution)/shard_map/ppermute | solution.py:300
  60.9 1.7 %collective-permute-done.1.other_ref = bf16[2,640,256]{2,1,0:T(8,128)(2,1)S(1)} collective-permute-done((bf16[2,640,256]{2,1,0:T(8,128)(2,1)S(1)}, bf16[2,640,256]{2,1,0:T(8,128)(2,1)S(1)}, u32[]{:S(2)}, u32[]{:S(2)}) %collective-permute-start.1) | collective-permute-done | bytes 655392 | tf_op jit(solution)/shard_map/ppermute | solution.py:300
  63.1 1.1 %cross.4 = bf16[2,256,256]{2,1,0:T(8,128)(2,1)S(1)} custom-call(s32[2,8]{1,0:T(2,128)S(1)} %copy-done, s32[2]{0:T(128)S(1)} %pad_add_fusion.place_ref, bf16[8,640,256]{2,1,0:T(8,128)(2,1)S(1)} %bitcast.6, bf16[2,640,256]{2,1,0:T(8,128)(2,1)S(1)} %collective-permute-done.1.other_ref), custom_call_target="tpu_custom_call" | custom-call | flops 335544320 | bytes 1572864 | tf_op jit(solution)/shard_map/cross/pallas_call | solution.py:232
  64.2 3.0 %collective-permute-start.6 = (bf16[2,256,256]{2,1,0:T(8,128)(2,1)S(1)}, bf16[2,256,256]{2,1,0:T(8,128)(2,1)S(1)}, u32[]{:S(2)}, u32[]{:S(2)}) collective-permute-start(bf16[2,256,256]{2,1,0:T(8,128)(2,1)S(1)} %cross.4), channel_id=1, source_target_pairs={{0,16},{1,80},{16,0},{17,64},{32,48},{33,112},{48,32},{49,96},{64,... | collective-permute-start | bytes 786440 | tf_op jit(solution)/shard_map/ppermute | solution.py:316
  67.5 1.8 %cross.5 = (bf16[2,256,256]{2,1,0:T(8,128)(2,1)S(1)}, bf16[2,256,256]{2,1,0:T(8,128)(2,1)S(1)}, bf16[2,256,256]{2,1,0:T(8,128)(2,1)S(1)}) custom-call(s32[2,8]{1,0:T(2,128)S(1)} %copy-done, s32[2]{0:T(128)S(1)} %pad_add_fusion.place_ref, bf16[8,640,256]{2,1,0:T(8,128)(2,1)S(1)} %bitcast.7, bf16[8,640,256]{2,1,0:T(8,128)(2,1)S(1)} %collective-permute-done.2.other_ref), custom_call_target="tpu_custom_call" | custom-call | flops 1006632960 | bytes 4718592 | tf_op jit(solution)/shard_map/cross/pallas_call | solution.py:232
  69.3 1.4 %collective-permute-start.7 = (bf16[2,256,256]{2,1,0:T(8,128)(2,1)S(1)}, bf16[2,256,256]{2,1,0:T(8,128)(2,1)S(1)}, u32[]{:S(2)}, u32[]{:S(2)}) collective-permute-start(bf16[2,256,256]{2,1,0:T(8,128)(2,1)S(1)} %get-tuple-element.53), channel_id=1, source_target_pairs={{0,48},{1,112},{16,32},{17,96},{32,16},{33,80},{48,0},{49,64},{64,... | collective-permute-start | bytes 786440 | tf_op jit(solution)/shard_map/ppermute | solution.py:316
  70.7 2.1 %collective-permute-start.8 = (bf16[2,256,256]{2,1,0:T(8,128)(2,1)S(1)}, bf16[2,256,256]{2,1,0:T(8,128)(2,1)S(1)}, u32[]{:S(2)}, u32[]{:S(2)}) collective-permute-start(bf16[2,256,256]{2,1,0:T(8,128)(2,1)S(1)} %get-tuple-element.54), channel_id=1, source_target_pairs={{0,32},{1,96},{16,48},{17,112},{32,0},{33,64},{48,16},{49,80},{64,... | collective-permute-start | bytes 786440 | tf_op jit(solution)/shard_map/ppermute | solution.py:316
  72.8 1.5 %collective-permute-start.9 = (bf16[2,256,256]{2,1,0:T(8,128)(2,1)S(1)}, bf16[2,256,256]{2,1,0:T(8,128)(2,1)S(1)}, u32[]{:S(2)}, u32[]{:S(2)}) collective-permute-start(bf16[2,256,256]{2,1,0:T(8,128)(2,1)S(1)} %get-tuple-element.55), channel_id=1, source_target_pairs={{0,80},{1,16},{16,64},{17,0},{32,112},{33,48},{48,96},{49,32},{64,... | collective-permute-start | bytes 786440 | tf_op jit(solution)/shard_map/ppermute | solution.py:316
  74.4 1.4 %cross.6 = (bf16[2,256,256]{2,1,0:T(8,128)(2,1)S(1)}, bf16[2,256,256]{2,1,0:T(8,128)(2,1)S(1)}) custom-call(s32[2,8]{1,0:T(2,128)S(1)} %copy-done, s32[2]{0:T(128)S(1)} %pad_add_fusion.place_ref, bf16[8,640,256]{2,1,0:T(8,128)(2,1)S(1)} %bitcast.8, bf16[8,640,256]{2,1,0:T(8,128)(2,1)S(1)} %collective-permute-done.2.other_ref), custom_call_target="tpu_custom_call" | custom-call | flops 671088640 | bytes 3145728 | tf_op jit(solution)/shard_map/cross/pallas_call | solution.py:232
  75.8 0.9 collective-permute-start.3
  76.7 1.4 %cross.7 = (bf16[2,256,256]{2,1,0:T(8,128)(2,1)S(1)}, bf16[2,256,256]{2,1,0:T(8,128)(2,1)S(1)}) custom-call(s32[2,8]{1,0:T(2,128)S(1)} %copy-done, s32[2]{0:T(128)S(1)} %pad_add_fusion.place_ref, bf16[8,640,256]{2,1,0:T(8,128)(2,1)S(1)} %bitcast.9, bf16[8,640,256]{2,1,0:T(8,128)(2,1)S(1)} %collective-permute-done.2.other_ref), custom_call_target="tpu_custom_call" | custom-call | flops 671088640 | bytes 3145728 | tf_op jit(solution)/shard_map/cross/pallas_call | solution.py:232
  78.2 3.3 %collective-permute-start.10 = (bf16[2,256,256]{2,1,0:T(8,128)(2,1)S(1)}, bf16[2,256,256]{2,1,0:T(8,128)(2,1)S(1)}, u32[]{:S(2)}, u32[]{:S(2)}) collective-permute-start(bf16[2,256,256]{2,1,0:T(8,128)(2,1)S(1)} %get-tuple-element.56), channel_id=1, source_target_pairs={{0,112},{1,48},{16,96},{17,32},{32,80},{33,16},{48,64},{49,0},{64,... | collective-permute-start | bytes 786440 | tf_op jit(solution)/shard_map/ppermute | solution.py:316
  81.5 3.5 %collective-permute-start.4 = (bf16[2,256,256]{2,1,0:T(8,128)(2,1)S(1)}, bf16[2,256,256]{2,1,0:T(8,128)(2,1)S(1)}, u32[]{:S(2)}, u32[]{:S(2)}) collective-permute-start(bf16[2,256,256]{2,1,0:T(8,128)(2,1)S(1)} %get-tuple-element.50), channel_id=1, source_target_pairs={{0,0},{1,64},{16,16},{17,80},{32,32},{33,96},{48,48},{49,112},{64,... | collective-permute-start | bytes 786440 | tf_op jit(solution)/shard_map/ppermute | solution.py:316
  85.0 1.9 %collective-permute-start.5 = (bf16[2,256,256]{2,1,0:T(8,128)(2,1)S(1)}, bf16[2,256,256]{2,1,0:T(8,128)(2,1)S(1)}, u32[]{:S(2)}, u32[]{:S(2)}) collective-permute-start(bf16[2,256,256]{2,1,0:T(8,128)(2,1)S(1)} %get-tuple-element.51), channel_id=1, source_target_pairs={{0,64},{1,0},{16,80},{17,16},{32,96},{33,32},{48,112},{49,48},{64,... | collective-permute-start | bytes 786440 | tf_op jit(solution)/shard_map/ppermute | solution.py:316
  86.9 3.8 %collective-permute-done.10.refs_4_ = bf16[2,256,256]{2,1,0:T(8,128)(2,1)S(1)} collective-permute-done((bf16[2,256,256]{2,1,0:T(8,128)(2,1)S(1)}, bf16[2,256,256]{2,1,0:T(8,128)(2,1)S(1)}, u32[]{:S(2)}, u32[]{:S(2)}) %collective-permute-start.10) | collective-permute-done | bytes 262176 | tf_op jit(solution)/shard_map/ppermute | solution.py:316
  90.7 2.1 %join.2.refs_3_ = f32[4,2,2,256,256]{4,3,2,1,0:T(8,128)} custom-call(s32[2]{0:T(128)S(1)} %pad_add_fusion.place_ref, bf16[2,256,256]{2,1,0:T(8,128)(2,1)S(1)} %collective-permute-done.6.refs_0_, bf16[2,256,256]{2,1,0:T(8,128)(2,1)S(1)} %collective-permute-done.7.refs_1_, bf16[2,256,256]{2,1,0:T(8,128)(2,1)S(1)} %collective-permute-done.8.refs_2_, ...), custom_call_target="tpu_custom_call" | custom-call | bytes 3932160 | tf_op jit(solution)/shard_map/join/pallas_call | solution.py:263
  92.8 2.0 %collective-permute-done.5.refs_2_ = bf16[2,256,256]{2,1,0:T(8,128)(2,1)S(1)} collective-permute-done((bf16[2,256,256]{2,1,0:T(8,128)(2,1)S(1)}, bf16[2,256,256]{2,1,0:T(8,128)(2,1)S(1)}, u32[]{:S(2)}, u32[]{:S(2)}) %collective-permute-start.5) | collective-permute-done | bytes 262176 | tf_op jit(solution)/shard_map/ppermute | solution.py:316
  94.8 1.7 %join.3 = f32[4,2,2,256,256]{4,3,2,1,0:T(8,128)} custom-call(s32[2]{0:T(128)S(1)} %pad_add_fusion.place_ref, bf16[2,256,256]{2,1,0:T(8,128)(2,1)S(1)} %collective-permute-done.3.refs_0_, bf16[2,256,256]{2,1,0:T(8,128)(2,1)S(1)} %collective-permute-done.4.refs_1_, ...), custom_call_target="tpu_custom_call", output_to_operand_aliasing={{}: (4, {})} | custom-call | bytes 2359296 | tf_op jit(solution)/shard_map/join/pallas_call | solution.py:263
  (15 shorter events, 1.5 us)
Async XLA Ops:
  0.8 6.0 %collective-permute-start = (bf16[256,128]{1,0:T(8,128)(2,1)S(1)}, bf16[256,128]{1,0:T(8,128)(2,1)S(1)}, u32[]{:S(2)}, u32[]{:S(2)}) collective-permute-start(bf16[256,128]{1,0:T(8,128)(2,1)S(1)} %slice.3), channel_id=1, source_target_pairs={{0,1},{1,2},{2,3},{3,4},{4,5},{5,6},{6,7},{7,8},{8,9},{9,10},{10,1... | collective-permute-start | bytes 196616 | tf_op jit(solution)/shard_map/ppermute | solution.py:288
  13.0 10.9 %copy-start = (s32[2,8]{1,0:T(2,128)S(1)}, s32[2,8]{1,0:T(2,128)}, u32[]{:S(2)}) copy-start(s32[2,8]{1,0:T(2,128)} %plan_ref.7) | copy-start | bytes 196
  13.0 43.8 %all-to-all-start = ((bf16[64,80,256]{2,1,0:T(8,128)(2,1)}), bf16[64,80,256]{2,1,0:T(8,128)(2,1)S(1)}, u32[]{:S(2)}, u32[]{:S(2)}) async-start(bf16[64,80,256]{2,1,0:T(8,128)(2,1)} %spectra.1), calls=%async_computation | async-start | bytes 5242880 | tf_op jit(solution)/shard_map/all_to_all | solution.py:294
  56.9 5.7 %collective-permute-start.1 = (bf16[2,640,256]{2,1,0:T(8,128)(2,1)S(1)}, bf16[2,640,256]{2,1,0:T(8,128)(2,1)S(1)}, u32[]{:S(2)}, u32[]{:S(2)}) collective-permute-start(bf16[2,640,256]{2,1,0:T(8,128)(2,1)S(1)} %pad_maximum_fusion), channel_id=1, source_target_pairs={{0,1},{1,0},{2,3},{3,2},{4,5},{5,4},{6,7},{7,6},{8,9},{9,8},{10,11... | collective-permute-start | bytes 1966088 | tf_op jit(solution)/shard_map/ppermute | solution.py:300
  62.6 4.9 %collective-permute-start.2 = (bf16[8,640,256]{2,1,0:T(8,128)(2,1)S(1)}, bf16[8,640,256]{2,1,0:T(8,128)(2,1)S(1)}, u32[]{:S(2)}, u32[]{:S(2)}) collective-permute-start(bf16[8,640,256]{2,1,0:T(8,128)(2,1)S(1)} %bitcast.5), channel_id=1, source_target_pairs={{0,1},{1,0},{2,3},{3,2},{4,5},{5,4},{6,7},{7,6},{8,9},{9,8},{10,11... | collective-permute-start | bytes 7864328 | tf_op jit(solution)/shard_map/ppermute | solution.py:302
  64.2 14.0 %collective-permute-start.6 = (bf16[2,256,256]{2,1,0:T(8,128)(2,1)S(1)}, bf16[2,256,256]{2,1,0:T(8,128)(2,1)S(1)}, u32[]{:S(2)}, u32[]{:S(2)}) collective-permute-start(bf16[2,256,256]{2,1,0:T(8,128)(2,1)S(1)} %cross.4), channel_id=1, source_target_pairs={{0,16},{1,80},{16,0},{17,64},{32,48},{33,112},{48,32},{49,96},{64,... | collective-permute-start | bytes 786440 | tf_op jit(solution)/shard_map/ppermute | solution.py:316
  69.3 12.2 %collective-permute-start.7 = (bf16[2,256,256]{2,1,0:T(8,128)(2,1)S(1)}, bf16[2,256,256]{2,1,0:T(8,128)(2,1)S(1)}, u32[]{:S(2)}, u32[]{:S(2)}) collective-permute-start(bf16[2,256,256]{2,1,0:T(8,128)(2,1)S(1)} %get-tuple-element.53), channel_id=1, source_target_pairs={{0,48},{1,112},{16,32},{17,96},{32,16},{33,80},{48,0},{49,64},{64,... | collective-permute-start | bytes 786440 | tf_op jit(solution)/shard_map/ppermute | solution.py:316
  70.7 14.3 %collective-permute-start.8 = (bf16[2,256,256]{2,1,0:T(8,128)(2,1)S(1)}, bf16[2,256,256]{2,1,0:T(8,128)(2,1)S(1)}, u32[]{:S(2)}, u32[]{:S(2)}) collective-permute-start(bf16[2,256,256]{2,1,0:T(8,128)(2,1)S(1)} %get-tuple-element.54), channel_id=1, source_target_pairs={{0,32},{1,96},{16,48},{17,112},{32,0},{33,64},{48,16},{49,80},{64,... | collective-permute-start | bytes 786440 | tf_op jit(solution)/shard_map/ppermute | solution.py:316
  72.8 14.1 %collective-permute-start.9 = (bf16[2,256,256]{2,1,0:T(8,128)(2,1)S(1)}, bf16[2,256,256]{2,1,0:T(8,128)(2,1)S(1)}, u32[]{:S(2)}, u32[]{:S(2)}) collective-permute-start(bf16[2,256,256]{2,1,0:T(8,128)(2,1)S(1)} %get-tuple-element.55), channel_id=1, source_target_pairs={{0,80},{1,16},{16,64},{17,0},{32,112},{33,48},{48,96},{49,32},{64,... | collective-permute-start | bytes 786440 | tf_op jit(solution)/shard_map/ppermute | solution.py:316
  75.8 17.0 %collective-permute-start.3 = (bf16[2,256,256]{2,1,0:T(8,128)(2,1)S(1)}, bf16[2,256,256]{2,1,0:T(8,128)(2,1)S(1)}, u32[]{:S(2)}, u32[]{:S(2)}) collective-permute-start(bf16[2,256,256]{2,1,0:T(8,128)(2,1)S(1)} %get-tuple-element.45), channel_id=1, source_target_pairs={{0,96},{1,32},{16,112},{17,48},{32,64},{33,0},{48,80},{49,16},{64,... | collective-permute-start | bytes 786440 | tf_op jit(solution)/shard_map/ppermute | solution.py:316
  78.2 12.5 %collective-permute-start.10 = (bf16[2,256,256]{2,1,0:T(8,128)(2,1)S(1)}, bf16[2,256,256]{2,1,0:T(8,128)(2,1)S(1)}, u32[]{:S(2)}, u32[]{:S(2)}) collective-permute-start(bf16[2,256,256]{2,1,0:T(8,128)(2,1)S(1)} %get-tuple-element.56), channel_id=1, source_target_pairs={{0,112},{1,48},{16,96},{17,32},{32,80},{33,16},{48,64},{49,0},{64,... | collective-permute-start | bytes 786440 | tf_op jit(solution)/shard_map/ppermute | solution.py:316
  81.5 11.4 %collective-permute-start.4 = (bf16[2,256,256]{2,1,0:T(8,128)(2,1)S(1)}, bf16[2,256,256]{2,1,0:T(8,128)(2,1)S(1)}, u32[]{:S(2)}, u32[]{:S(2)}) collective-permute-start(bf16[2,256,256]{2,1,0:T(8,128)(2,1)S(1)} %get-tuple-element.50), channel_id=1, source_target_pairs={{0,0},{1,64},{16,16},{17,80},{32,32},{33,96},{48,48},{49,112},{64,... | collective-permute-start | bytes 786440 | tf_op jit(solution)/shard_map/ppermute | solution.py:316
  85.0 9.8 %collective-permute-start.5 = (bf16[2,256,256]{2,1,0:T(8,128)(2,1)S(1)}, bf16[2,256,256]{2,1,0:T(8,128)(2,1)S(1)}, u32[]{:S(2)}, u32[]{:S(2)}) collective-permute-start(bf16[2,256,256]{2,1,0:T(8,128)(2,1)S(1)} %get-tuple-element.51), channel_id=1, source_target_pairs={{0,64},{1,0},{16,80},{17,16},{32,96},{33,32},{48,112},{49,48},{64,... | collective-permute-start | bytes 786440 | tf_op jit(solution)/shard_map/ppermute | solution.py:316

commit v6 on v5

--- a/solution.py
+++ b/solution.py
@@ -134,6 +134,10 @@
         at = rows_of(group)
         return pltpu.make_async_copy(white_ref.at[:, at, :], out_ref.at[:, at, :], out_sems.at[group])
 
+    def send_part(group, part):
+        at = (pl.ds(part * TILE, TILE), rows_of(group), slice(None))
+        return pltpu.make_async_copy(white_ref.at[at], out_ref.at[at], out_sems.at[group + part])
+
     def make(samples_at):
         carry = carry_ref[...]
         for inner in range(STEP_WINDOWS):
@@ -145,7 +149,7 @@
             held_ref[inner] = (stacked * (1.0 / jnp.sqrt(power))).astype(jnp.bfloat16)
         carry_ref[...] = carry
 
-    def place(group):
+    def place(group, sent=False):
         for part in range(F // TILE):
             rows = []
             for inner in range(STEP_WINDOWS):
@@ -156,6 +160,8 @@
             ).astype(jnp.bfloat16)
             for n in range(TILE):
                 white_ref[part * TILE + n, rows_of(group), :] = placed[n * TILE : (n + 1) * TILE]
+            if sent:
+                send_part(group, part).start()
 
     for group in range(1, groups):
         fetch(group).start()
@@ -169,10 +175,11 @@
         make(samples_ref.at[group - 1])
         send(group - 1).start()
 
-    place(groups - 1)
-    send(groups - 1).start()
-    for group in range(groups):
+    place(groups - 1, sent=True)
+    for group in range(groups - 1):
         send(group).wait()
+    for part in range(F // TILE):
+        send_part(groups - 1, part).wait()
 
 
 def spectra(tail, tables, records):
@@ -190,7 +197,7 @@
             pltpu.VMEM((STEP_WINDOWS, 2 * F, channels), jnp.bfloat16),
             pltpu.VMEM(result, jnp.bfloat16),
             pltpu.SemaphoreType.DMA((groups - 1,)),
-            pltpu.SemaphoreType.DMA((groups,)),
+            pltpu.SemaphoreType.DMA((groups - 1 + F // TILE,)),
         ],
         compiler_params=pltpu.CompilerParams(vmem_limit_bytes=VMEM),
         name="spectra",

time: 96.9 us -> 96.8 us (level)
  no operation moved by 1% of the time
where the time goes in v6:
time: 96.8 us; the launch traced here: 96.5 us
  waiting for transfers between devices  38.5 us (40%)
  starting transfers between devices  37.5 us (39%)
  Pallas kernels  17 us (18%)
  between operations  1.87 us (2%)
  local copies, waits for them, and re-layouts  1.48 us (2%)
    all_to_all x1, waiting for transfers between devices, on_device(): here = lax.all_to_all(white, ('chan', 'chip'), 0, 0, tiled=True)  30.6 us
    ppermute x8, starting transfers between devices, on_device(): parts.append(lax.ppermute(product, ('chan', 'core'), route))  17.7 us
    all_to_all x1, starting transfers between devices, on_device(): here = lax.all_to_all(white, ('chan', 'chip'), 0, 0, tiled=True)  10.9 us
    pallas_call x1, Pallas kernels, spectra(): pl.pallas_call(spectra_kernel, out_shape=pltpu.HBM(result, jnp.bfloat16),...  6.07 us
    ppermute x8, waiting for transfers between devices, on_device(): parts.append(lax.ppermute(product, ('chan', 'core'), route))  5.75 us
    pallas_call x4, Pallas kernels, cross(): pl.pallas_call(functools.partial(cross_kernel, scale, steps), in_specs=[I...  5.71 us
    ppermute x1, starting transfers between devices, on_device(): lax.ppermute(records[:, samples_here - WL // 2:], ('chip', 'core'), [(i,...  4.58 us
    ppermute x1, starting transfers between devices, on_device(): first_other = lax.ppermute(jnp.stack(away), 'core', swap)  3.97 us
  transfers between devices with their start and end apart: 12, of which 5 were waited for; matrix products, arithmetic and copies ran while one was open for 1% of the time, Pallas kernels for 10%

profile of v6, /device:TPU:1, one launch (start us, length us, event | category | flops | bytes accessed | tf_op | source)
XLA Modules:
  0.0 96.5 jit_solution(7230252978894416908)
XLA Ops:
  0.0 0.8 slice.3
  0.8 4.6 %collective-permute-start = (bf16[256,128]{1,0:T(8,128)(2,1)S(1)}, bf16[256,128]{1,0:T(8,128)(2,1)S(1)}, u32[]{:S(2)}, u32[]{:S(2)}) collective-permute-start(bf16[256,128]{1,0:T(8,128)(2,1)S(1)} %slice.3), channel_id=1, source_target_pairs={{0,1},{1,2},{2,3},{3,4},{4,5},{5,6},{6,7},{7,8},{8,9},{9,10},{10,1... | collective-permute-start | bytes 196616 | tf_op jit(solution)/shard_map/ppermute | solution.py:295
  5.4 1.4 %table.1 = (bf16[384,256]{1,0:T(8,128)(2,1)S(1)}, bf16[128,256]{1,0:T(8,128)(2,1)S(1)}, bf16[256,256]{1,0:T(8,128)(2,1)S(1)}, bf16[256,2048]{1,0:T(8,128)(2,1)S(1)}) custom-call(f32[64]{0:T(128)} %taps_at.1, f32[128,256]{1,0:T(8,128)} %constant.23.clone.dft_at, bf16[256,10240]{1,0:T(8,128)(2,1)} %records_ref.3), custom_call_target="tpu_custom_call" | custom-call | tf_op jit(solution)/shard_map/table/pallas_call | solution.py:86
  6.9 6.1 %spectra.1 = bf16[64,80,256]{2,1,0:T(8,128)(2,1)} custom-call(bf16[256,128]{1,0:T(8,128)(2,1)S(1)} %collective-permute-done.tail_ref, bf16[384,256]{1,0:T(8,128)(2,1)S(1)} %get-tuple-element.31.main_ref, bf16[128,256]{1,0:T(8,128)(2,1)S(1)} %get-tuple-element.32.before_ref, bf16[256,256]{1,0:T(8,128)(2,1)S(1)} %get-tuple-element.33.order_ref, ...), custom_call_target="tpu_custom_call" | custom-call | tf_op jit(solution)/shard_map/spectra/pallas_call | solution.py:189
  13.0 10.9 %all-to-all-start = ((bf16[64,80,256]{2,1,0:T(8,128)(2,1)}), bf16[64,80,256]{2,1,0:T(8,128)(2,1)S(1)}, u32[]{:S(2)}, u32[]{:S(2)}) async-start(bf16[64,80,256]{2,1,0:T(8,128)(2,1)} %spectra.1), calls=%async_computation | async-start | bytes 5242880 | tf_op jit(solution)/shard_map/all_to_all | solution.py:301
  26.1 30.6 %all-to-all-done = bf16[64,80,256]{2,1,0:T(8,128)(2,1)S(1)} async-done(((bf16[64,80,256]{2,1,0:T(8,128)(2,1)}), bf16[64,80,256]{2,1,0:T(8,128)(2,1)S(1)}, u32[]{:S(2)}, u32[]{:S(2)}) %all-to-all-start) | async-done | bytes 2621472 | tf_op jit(solution)/shard_map/all_to_all | solution.py:301
  56.9 4.0 %collective-permute-start.1 = (bf16[2,640,256]{2,1,0:T(8,128)(2,1)S(1)}, bf16[2,640,256]{2,1,0:T(8,128)(2,1)S(1)}, u32[]{:S(2)}, u32[]{:S(2)}) collective-permute-start(bf16[2,640,256]{2,1,0:T(8,128)(2,1)S(1)} %pad_maximum_fusion), channel_id=1, source_target_pairs={{0,1},{1,0},{2,3},{3,2},{4,5},{5,4},{6,7},{7,6},{8,9},{9,8},{10,11... | collective-permute-start | bytes 1966088 | tf_op jit(solution)/shard_map/ppermute | solution.py:307
  60.8 1.7 %collective-permute-done.1.other_ref = bf16[2,640,256]{2,1,0:T(8,128)(2,1)S(1)} collective-permute-done((bf16[2,640,256]{2,1,0:T(8,128)(2,1)S(1)}, bf16[2,640,256]{2,1,0:T(8,128)(2,1)S(1)}, u32[]{:S(2)}, u32[]{:S(2)}) %collective-permute-start.1) | collective-permute-done | bytes 655392 | tf_op jit(solution)/shard_map/ppermute | solution.py:307
  63.0 1.1 %cross.4 = bf16[2,256,256]{2,1,0:T(8,128)(2,1)S(1)} custom-call(s32[2,8]{1,0:T(2,128)S(1)} %copy-done, s32[2]{0:T(128)S(1)} %pad_add_fusion.place_ref, bf16[8,640,256]{2,1,0:T(8,128)(2,1)S(1)} %bitcast.6, bf16[2,640,256]{2,1,0:T(8,128)(2,1)S(1)} %collective-permute-done.1.other_ref), custom_call_target="tpu_custom_call" | custom-call | flops 335544320 | bytes 1572864 | tf_op jit(solution)/shard_map/cross/pallas_call | solution.py:239
  64.1 3.0 %collective-permute-start.6 = (bf16[2,256,256]{2,1,0:T(8,128)(2,1)S(1)}, bf16[2,256,256]{2,1,0:T(8,128)(2,1)S(1)}, u32[]{:S(2)}, u32[]{:S(2)}) collective-permute-start(bf16[2,256,256]{2,1,0:T(8,128)(2,1)S(1)} %cross.4), channel_id=1, source_target_pairs={{0,16},{1,80},{16,0},{17,64},{32,48},{33,112},{48,32},{49,96},{64,... | collective-permute-start | bytes 786440 | tf_op jit(solution)/shard_map/ppermute | solution.py:323
  67.5 1.8 %cross.5 = (bf16[2,256,256]{2,1,0:T(8,128)(2,1)S(1)}, bf16[2,256,256]{2,1,0:T(8,128)(2,1)S(1)}, bf16[2,256,256]{2,1,0:T(8,128)(2,1)S(1)}) custom-call(s32[2,8]{1,0:T(2,128)S(1)} %copy-done, s32[2]{0:T(128)S(1)} %pad_add_fusion.place_ref, bf16[8,640,256]{2,1,0:T(8,128)(2,1)S(1)} %bitcast.7, bf16[8,640,256]{2,1,0:T(8,128)(2,1)S(1)} %collective-permute-done.2.other_ref), custom_call_target="tpu_custom_call" | custom-call | flops 1006632960 | bytes 4718592 | tf_op jit(solution)/shard_map/cross/pallas_call | solution.py:239
  69.3 1.4 %collective-permute-start.7 = (bf16[2,256,256]{2,1,0:T(8,128)(2,1)S(1)}, bf16[2,256,256]{2,1,0:T(8,128)(2,1)S(1)}, u32[]{:S(2)}, u32[]{:S(2)}) collective-permute-start(bf16[2,256,256]{2,1,0:T(8,128)(2,1)S(1)} %get-tuple-element.53), channel_id=1, source_target_pairs={{0,48},{1,112},{16,32},{17,96},{32,16},{33,80},{48,0},{49,64},{64,... | collective-permute-start | bytes 786440 | tf_op jit(solution)/shard_map/ppermute | solution.py:323
  70.7 2.1 %collective-permute-start.8 = (bf16[2,256,256]{2,1,0:T(8,128)(2,1)S(1)}, bf16[2,256,256]{2,1,0:T(8,128)(2,1)S(1)}, u32[]{:S(2)}, u32[]{:S(2)}) collective-permute-start(bf16[2,256,256]{2,1,0:T(8,128)(2,1)S(1)} %get-tuple-element.54), channel_id=1, source_target_pairs={{0,32},{1,96},{16,48},{17,112},{32,0},{33,64},{48,16},{49,80},{64,... | collective-permute-start | bytes 786440 | tf_op jit(solution)/shard_map/ppermute | solution.py:323
  72.8 1.5 %collective-permute-start.9 = (bf16[2,256,256]{2,1,0:T(8,128)(2,1)S(1)}, bf16[2,256,256]{2,1,0:T(8,128)(2,1)S(1)}, u32[]{:S(2)}, u32[]{:S(2)}) collective-permute-start(bf16[2,256,256]{2,1,0:T(8,128)(2,1)S(1)} %get-tuple-element.55), channel_id=1, source_target_pairs={{0,80},{1,16},{16,64},{17,0},{32,112},{33,48},{48,96},{49,32},{64,... | collective-permute-start | bytes 786440 | tf_op jit(solution)/shard_map/ppermute | solution.py:323
  74.3 1.4 %cross.6 = (bf16[2,256,256]{2,1,0:T(8,128)(2,1)S(1)}, bf16[2,256,256]{2,1,0:T(8,128)(2,1)S(1)}) custom-call(s32[2,8]{1,0:T(2,128)S(1)} %copy-done, s32[2]{0:T(128)S(1)} %pad_add_fusion.place_ref, bf16[8,640,256]{2,1,0:T(8,128)(2,1)S(1)} %bitcast.8, bf16[8,640,256]{2,1,0:T(8,128)(2,1)S(1)} %collective-permute-done.2.other_ref), custom_call_target="tpu_custom_call" | custom-call | flops 671088640 | bytes 3145728 | tf_op jit(solution)/shard_map/cross/pallas_call | solution.py:239
  75.7 0.9 collective-permute-start.3
  76.7 1.4 %cross.7 = (bf16[2,256,256]{2,1,0:T(8,128)(2,1)S(1)}, bf16[2,256,256]{2,1,0:T(8,128)(2,1)S(1)}) custom-call(s32[2,8]{1,0:T(2,128)S(1)} %copy-done, s32[2]{0:T(128)S(1)} %pad_add_fusion.place_ref, bf16[8,640,256]{2,1,0:T(8,128)(2,1)S(1)} %bitcast.9, bf16[8,640,256]{2,1,0:T(8,128)(2,1)S(1)} %collective-permute-done.2.other_ref), custom_call_target="tpu_custom_call" | custom-call | flops 671088640 | bytes 3145728 | tf_op jit(solution)/shard_map/cross/pallas_call | solution.py:239
  78.1 3.3 %collective-permute-start.10 = (bf16[2,256,256]{2,1,0:T(8,128)(2,1)S(1)}, bf16[2,256,256]{2,1,0:T(8,128)(2,1)S(1)}, u32[]{:S(2)}, u32[]{:S(2)}) collective-permute-start(bf16[2,256,256]{2,1,0:T(8,128)(2,1)S(1)} %get-tuple-element.56), channel_id=1, source_target_pairs={{0,112},{1,48},{16,96},{17,32},{32,80},{33,16},{48,64},{49,0},{64,... | collective-permute-start | bytes 786440 | tf_op jit(solution)/shard_map/ppermute | solution.py:323
  81.4 3.5 %collective-permute-start.4 = (bf16[2,256,256]{2,1,0:T(8,128)(2,1)S(1)}, bf16[2,256,256]{2,1,0:T(8,128)(2,1)S(1)}, u32[]{:S(2)}, u32[]{:S(2)}) collective-permute-start(bf16[2,256,256]{2,1,0:T(8,128)(2,1)S(1)} %get-tuple-element.50), channel_id=1, source_target_pairs={{0,0},{1,64},{16,16},{17,80},{32,32},{33,96},{48,48},{49,112},{64,... | collective-permute-start | bytes 786440 | tf_op jit(solution)/shard_map/ppermute | solution.py:323
  84.9 1.9 %collective-permute-start.5 = (bf16[2,256,256]{2,1,0:T(8,128)(2,1)S(1)}, bf16[2,256,256]{2,1,0:T(8,128)(2,1)S(1)}, u32[]{:S(2)}, u32[]{:S(2)}) collective-permute-start(bf16[2,256,256]{2,1,0:T(8,128)(2,1)S(1)} %get-tuple-element.51), channel_id=1, source_target_pairs={{0,64},{1,0},{16,80},{17,16},{32,96},{33,32},{48,112},{49,48},{64,... | collective-permute-start | bytes 786440 | tf_op jit(solution)/shard_map/ppermute | solution.py:323
  86.9 3.8 %collective-permute-done.10.refs_4_ = bf16[2,256,256]{2,1,0:T(8,128)(2,1)S(1)} collective-permute-done((bf16[2,256,256]{2,1,0:T(8,128)(2,1)S(1)}, bf16[2,256,256]{2,1,0:T(8,128)(2,1)S(1)}, u32[]{:S(2)}, u32[]{:S(2)}) %collective-permute-start.10) | collective-permute-done | bytes 262176 | tf_op jit(solution)/shard_map/ppermute | solution.py:323
  90.7 2.1 %join.2.refs_3_ = f32[4,2,2,256,256]{4,3,2,1,0:T(8,128)} custom-call(s32[2]{0:T(128)S(1)} %pad_add_fusion.place_ref, bf16[2,256,256]{2,1,0:T(8,128)(2,1)S(1)} %collective-permute-done.6.refs_0_, bf16[2,256,256]{2,1,0:T(8,128)(2,1)S(1)} %collective-permute-done.7.refs_1_, bf16[2,256,256]{2,1,0:T(8,128)(2,1)S(1)} %collective-permute-done.8.refs_2_, ...), custom_call_target="tpu_custom_call" | custom-call | bytes 3932160 | tf_op jit(solution)/shard_map/join/pallas_call | solution.py:270
  92.8 2.0 %collective-permute-done.5.refs_2_ = bf16[2,256,256]{2,1,0:T(8,128)(2,1)S(1)} collective-permute-done((bf16[2,256,256]{2,1,0:T(8,128)(2,1)S(1)}, bf16[2,256,256]{2,1,0:T(8,128)(2,1)S(1)}, u32[]{:S(2)}, u32[]{:S(2)}) %collective-permute-start.5) | collective-permute-done | bytes 262176 | tf_op jit(solution)/shard_map/ppermute | solution.py:323
  94.8 1.7 %join.3 = f32[4,2,2,256,256]{4,3,2,1,0:T(8,128)} custom-call(s32[2]{0:T(128)S(1)} %pad_add_fusion.place_ref, bf16[2,256,256]{2,1,0:T(8,128)(2,1)S(1)} %collective-permute-done.3.refs_0_, bf16[2,256,256]{2,1,0:T(8,128)(2,1)S(1)} %collective-permute-done.4.refs_1_, ...), custom_call_target="tpu_custom_call", output_to_operand_aliasing={{}: (4, {})} | custom-call | bytes 2359296 | tf_op jit(solution)/shard_map/join/pallas_call | solution.py:270
  (15 shorter events, 1.5 us)
Async XLA Ops:
  0.8 6.0 %collective-permute-start = (bf16[256,128]{1,0:T(8,128)(2,1)S(1)}, bf16[256,128]{1,0:T(8,128)(2,1)S(1)}, u32[]{:S(2)}, u32[]{:S(2)}) collective-permute-start(bf16[256,128]{1,0:T(8,128)(2,1)S(1)} %slice.3), channel_id=1, source_target_pairs={{0,1},{1,2},{2,3},{3,4},{4,5},{5,6},{6,7},{7,8},{8,9},{9,10},{10,1... | collective-permute-start | bytes 196616 | tf_op jit(solution)/shard_map/ppermute | solution.py:295
  13.0 10.9 %copy-start = (s32[2,8]{1,0:T(2,128)S(1)}, s32[2,8]{1,0:T(2,128)}, u32[]{:S(2)}) copy-start(s32[2,8]{1,0:T(2,128)} %plan_ref.7) | copy-start | bytes 196
  13.0 43.8 %all-to-all-start = ((bf16[64,80,256]{2,1,0:T(8,128)(2,1)}), bf16[64,80,256]{2,1,0:T(8,128)(2,1)S(1)}, u32[]{:S(2)}, u32[]{:S(2)}) async-start(bf16[64,80,256]{2,1,0:T(8,128)(2,1)} %spectra.1), calls=%async_computation | async-start | bytes 5242880 | tf_op jit(solution)/shard_map/all_to_all | solution.py:301
  56.9 5.7 %collective-permute-start.1 = (bf16[2,640,256]{2,1,0:T(8,128)(2,1)S(1)}, bf16[2,640,256]{2,1,0:T(8,128)(2,1)S(1)}, u32[]{:S(2)}, u32[]{:S(2)}) collective-permute-start(bf16[2,640,256]{2,1,0:T(8,128)(2,1)S(1)} %pad_maximum_fusion), channel_id=1, source_target_pairs={{0,1},{1,0},{2,3},{3,2},{4,5},{5,4},{6,7},{7,6},{8,9},{9,8},{10,11... | collective-permute-start | bytes 1966088 | tf_op jit(solution)/shard_map/ppermute | solution.py:307
  62.6 4.9 %collective-permute-start.2 = (bf16[8,640,256]{2,1,0:T(8,128)(2,1)S(1)}, bf16[8,640,256]{2,1,0:T(8,128)(2,1)S(1)}, u32[]{:S(2)}, u32[]{:S(2)}) collective-permute-start(bf16[8,640,256]{2,1,0:T(8,128)(2,1)S(1)} %bitcast.5), channel_id=1, source_target_pairs={{0,1},{1,0},{2,3},{3,2},{4,5},{5,4},{6,7},{7,6},{8,9},{9,8},{10,11... | collective-permute-start | bytes 7864328 | tf_op jit(solution)/shard_map/ppermute | solution.py:309
  64.1 14.0 %collective-permute-start.6 = (bf16[2,256,256]{2,1,0:T(8,128)(2,1)S(1)}, bf16[2,256,256]{2,1,0:T(8,128)(2,1)S(1)}, u32[]{:S(2)}, u32[]{:S(2)}) collective-permute-start(bf16[2,256,256]{2,1,0:T(8,128)(2,1)S(1)} %cross.4), channel_id=1, source_target_pairs={{0,16},{1,80},{16,0},{17,64},{32,48},{33,112},{48,32},{49,96},{64,... | collective-permute-start | bytes 786440 | tf_op jit(solution)/shard_map/ppermute | solution.py:323
  69.3 12.2 %collective-permute-start.7 = (bf16[2,256,256]{2,1,0:T(8,128)(2,1)S(1)}, bf16[2,256,256]{2,1,0:T(8,128)(2,1)S(1)}, u32[]{:S(2)}, u32[]{:S(2)}) collective-permute-start(bf16[2,256,256]{2,1,0:T(8,128)(2,1)S(1)} %get-tuple-element.53), channel_id=1, source_target_pairs={{0,48},{1,112},{16,32},{17,96},{32,16},{33,80},{48,0},{49,64},{64,... | collective-permute-start | bytes 786440 | tf_op jit(solution)/shard_map/ppermute | solution.py:323
  70.7 14.3 %collective-permute-start.8 = (bf16[2,256,256]{2,1,0:T(8,128)(2,1)S(1)}, bf16[2,256,256]{2,1,0:T(8,128)(2,1)S(1)}, u32[]{:S(2)}, u32[]{:S(2)}) collective-permute-start(bf16[2,256,256]{2,1,0:T(8,128)(2,1)S(1)} %get-tuple-element.54), channel_id=1, source_target_pairs={{0,32},{1,96},{16,48},{17,112},{32,0},{33,64},{48,16},{49,80},{64,... | collective-permute-start | bytes 786440 | tf_op jit(solution)/shard_map/ppermute | solution.py:323
  72.8 14.1 %collective-permute-start.9 = (bf16[2,256,256]{2,1,0:T(8,128)(2,1)S(1)}, bf16[2,256,256]{2,1,0:T(8,128)(2,1)S(1)}, u32[]{:S(2)}, u32[]{:S(2)}) collective-permute-start(bf16[2,256,256]{2,1,0:T(8,128)(2,1)S(1)} %get-tuple-element.55), channel_id=1, source_target_pairs={{0,80},{1,16},{16,64},{17,0},{32,112},{33,48},{48,96},{49,32},{64,... | collective-permute-start | bytes 786440 | tf_op jit(solution)/shard_map/ppermute | solution.py:323
  75.7 17.0 %collective-permute-start.3 = (bf16[2,256,256]{2,1,0:T(8,128)(2,1)S(1)}, bf16[2,256,256]{2,1,0:T(8,128)(2,1)S(1)}, u32[]{:S(2)}, u32[]{:S(2)}) collective-permute-start(bf16[2,256,256]{2,1,0:T(8,128)(2,1)S(1)} %get-tuple-element.45), channel_id=1, source_target_pairs={{0,96},{1,32},{16,112},{17,48},{32,64},{33,0},{48,80},{49,16},{64,... | collective-permute-start | bytes 786440 | tf_op jit(solution)/shard_map/ppermute | solution.py:323
  78.1 12.5 %collective-permute-start.10 = (bf16[2,256,256]{2,1,0:T(8,128)(2,1)S(1)}, bf16[2,256,256]{2,1,0:T(8,128)(2,1)S(1)}, u32[]{:S(2)}, u32[]{:S(2)}) collective-permute-start(bf16[2,256,256]{2,1,0:T(8,128)(2,1)S(1)} %get-tuple-element.56), channel_id=1, source_target_pairs={{0,112},{1,48},{16,96},{17,32},{32,80},{33,16},{48,64},{49,0},{64,... | collective-permute-start | bytes 786440 | tf_op jit(solution)/shard_map/ppermute | solution.py:323
  81.4 11.4 %collective-permute-start.4 = (bf16[2,256,256]{2,1,0:T(8,128)(2,1)S(1)}, bf16[2,256,256]{2,1,0:T(8,128)(2,1)S(1)}, u32[]{:S(2)}, u32[]{:S(2)}) collective-permute-start(bf16[2,256,256]{2,1,0:T(8,128)(2,1)S(1)} %get-tuple-element.50), channel_id=1, source_target_pairs={{0,0},{1,64},{16,16},{17,80},{32,32},{33,96},{48,48},{49,112},{64,... | collective-permute-start | bytes 786440 | tf_op jit(solution)/shard_map/ppermute | solution.py:323
  84.9 9.8 %collective-permute-start.5 = (bf16[2,256,256]{2,1,0:T(8,128)(2,1)S(1)}, bf16[2,256,256]{2,1,0:T(8,128)(2,1)S(1)}, u32[]{:S(2)}, u32[]{:S(2)}) collective-permute-start(bf16[2,256,256]{2,1,0:T(8,128)(2,1)S(1)} %get-tuple-element.51), channel_id=1, source_target_pairs={{0,64},{1,0},{16,80},{17,16},{32,96},{33,32},{48,112},{49,48},{64,... | collective-permute-start | bytes 786440 | tf_op jit(solution)/shard_map/ppermute | solution.py:323
